TPU v7x, 256 devices: a whole 4x4x8 slice. The times are simulated.
256 devices in a mesh: section: 2 (over z_hi), dp: 4 (over x), expert: 32 (over y, z_lo, core).
Axes of the slice: x: 4, y: 4, z: 8 (z_hi: 2, z_lo: 4; z = z_hi * 4 + z_lo), core: 2. Of those that a mesh axis runs over, the one named last changes fastest.
Arguments:
- activations: bfloat16 [2, 16384, 4096], P('section', ('dp', 'expert')), may hold values from -6 to 6
- norm_gain: float32 [2, 4096], P('section'), may hold values from 0.25 to 1.75
- route_ids: int32 [2, 16384, 2], P('section', ('dp', 'expert')), may hold values from 0 to 15, all different within a row; in each aligned block of 128 rows (0 to 127, 128 to 255, ..., all dimensions but the last counted through in order) at most 18 rows name the same one
- route_gates: float32 [2, 16384, 2], P('section', ('dp', 'expert')), may hold values from 0.2 to 1
- gate_weight: bfloat16 [2, 4096, 12288], P('section', None, 'expert'), may hold values from -0.09375 to 0.09375
- up_weight: bfloat16 [2, 4096, 12288], P('section', None, 'expert'), may hold values from -0.09375 to 0.09375
- leak_rates: float32 [2, 12288], P('section', 'expert'), may hold values from 0.2 to 0.9
- down_weight: bfloat16 [2, 12288, 4096], P('section', 'expert', 'dp'), may hold values from -0.21875 to 0.21875
- cotangent: bfloat16 [2, 16384, 4096], P('section', ('dp', 'expert')), may hold values from -6 to 6
Outputs:
- passed_on: bfloat16 [2, 16384, 4096], P('section', ('dp', 'expert'))
- passed_back: bfloat16 [2, 16384, 4096], P('section', ('dp', 'expert'))
- up_grad: bfloat16 [2, 4096, 12288], P('section', 'dp', 'expert')
Inputs may be any that keep to these rules, and one draw needn't show every extreme that they name: `route_ids`: within one section, the 128 tokens of one device name each expert at most 18 times, and some device reaches 18 for some expert; the two experts of a token differ.
All inputs are finite; a program needn't handle non-finite values.
Results may differ from a plain program's by a relative error of at most 0.015.
Values may be sent and summed in bfloat16 or wider, within the bound.
A program may use at most 192 MiB of HBM per device.

v0:
```python
import jax
import jax.numpy as jnp
from jax import lax
from jax.sharding import PartitionSpec as P

TSTEPS = 4


EPS = 1e-06
THETA = 0.5
SHARP = 4.0


def passed_along(value, axis, steps):
    count = lax.axis_size(axis)
    leading, last = (max(0, -steps), min(count, count - steps))
    return lax.ppermute(value, axis, [(source, source + steps) for source in range(leading, last)])


def lif_rate(gate_act, up_act, leak_rate):
    drive = jax.nn.silu(gate_act) * up_act
    volts = jnp.zeros_like(drive)
    spike_sum = jnp.zeros_like(drive)
    for timestep in range(TSTEPS):
        volts = leak_rate * volts + drive
        spikes = jax.nn.sigmoid(SHARP * (volts - THETA)) - jax.nn.sigmoid(SHARP * (-volts - THETA))
        volts = volts - THETA * spikes
        spike_sum = spike_sum + spikes
    return spike_sum / TSTEPS


def to_experts(slot_rows):
    model_width = slot_rows.shape[2]
    doubled = jnp.repeat(slot_rows, 2, axis=0)
    gathered = lax.all_to_all(doubled, "expert", split_axis=0, concat_axis=0, tiled=True)
    return gathered.reshape(-1, model_width)


def from_experts(partials, experts, capacity):
    model_width = partials.shape[2]
    returned = lax.all_to_all(
        partials.astype(jnp.bfloat16), "expert", split_axis=0, concat_axis=0, tiled=True
    ).astype(partials.dtype)
    paired = returned.reshape(experts, 2, capacity, model_width)
    summed = jnp.sum(paired, axis=1).astype(jnp.bfloat16)
    return summed.reshape(experts * capacity, model_width).astype(jnp.float32)


def per_device(
    activations,
    norm_gain,
    route_ids,
    route_gates,
    gate_weight,
    up_weight,
    leak_rates,
    down_weight,
    cotangent,
):
    tok_count = activations.shape[1]
    model_width = activations.shape[2]
    experts = lax.axis_size("expert") // 2
    capacity = min(tok_count, 2 * (9 * tok_count // (8 * experts)))
    tokens = activations[0].astype(jnp.float32)
    gain_row = norm_gain[0]
    inv_rms = lax.rsqrt(jnp.mean(tokens * tokens, axis=-1, keepdims=True) + EPS)
    normed = (tokens * inv_rms * gain_row).astype(jnp.bfloat16)
    flat_ids = route_ids[0].reshape(-1)
    onehot = (flat_ids[:, None] == jnp.arange(experts, dtype=jnp.int32)[None, :]).astype(jnp.int32)
    slot_index = jnp.sum(onehot * (jnp.cumsum(onehot, axis=0) - 1), axis=1)
    places = (flat_ids * capacity + slot_index).reshape(tok_count, 2)
    positions = jnp.arange(experts * capacity, dtype=jnp.int32)[:, None]
    pick_first = positions == places[None, :, 0]
    pick_second = positions == places[None, :, 1]
    pick_both = jnp.logical_or(pick_first, pick_second)
    slot_rows = jnp.dot(
        pick_both.astype(jnp.bfloat16), normed, preferred_element_type=jnp.float32
    ).astype(jnp.bfloat16)
    arrived = to_experts(slot_rows.reshape(experts, capacity, model_width))
    gate_local = gate_weight[0]
    up_local = up_weight[0]
    leak_local = leak_rates[0]
    down_full = lax.all_gather(down_weight[0], "dp", axis=1, tiled=True)
    gate_act = jnp.dot(arrived, gate_local, preferred_element_type=jnp.float32)
    up_act = jnp.dot(arrived, up_local, preferred_element_type=jnp.float32)
    spike_rate = lif_rate(gate_act, up_act, leak_local).astype(jnp.bfloat16)
    out_part = jnp.dot(spike_rate, down_full, preferred_element_type=jnp.float32)
    expert_out = from_experts(out_part.reshape(-1, capacity, model_width), experts, capacity)
    weights = route_gates[0]
    mixing = jnp.where(pick_first.T, weights[:, 0:1], 0.0) + jnp.where(
        pick_second.T, weights[:, 1:2], 0.0
    )
    moe_sum = jnp.dot(
        mixing, expert_out, precision=lax.Precision.HIGHEST, preferred_element_type=jnp.float32
    )
    section_out = (tokens + moe_sum).astype(jnp.bfloat16)
    passed_on = passed_along(section_out[None], "section", 1)
    upstream = cotangent[0].astype(jnp.float32)
    grad_first = (weights[:, 0:1] * upstream).astype(jnp.bfloat16)
    grad_second = (weights[:, 1:2] * upstream).astype(jnp.bfloat16)
    grad_slots = jnp.dot(
        pick_first.astype(jnp.bfloat16), grad_first, preferred_element_type=jnp.float32
    )
    grad_slots = grad_slots + jnp.dot(
        pick_second.astype(jnp.bfloat16), grad_second, preferred_element_type=jnp.float32
    )
    grad_rows = to_experts(grad_slots.astype(jnp.bfloat16).reshape(experts, capacity, model_width))
    rate_grad = lax.dot_general(
        grad_rows, down_full, (((1,), (1,)), ((), ())), preferred_element_type=jnp.float32
    )
    unused_rate, pullback = jax.vjp(
        lambda gate_in, up_in: lif_rate(gate_in, up_in, leak_local), gate_act, up_act
    )
    gate_grad, up_act_grad = pullback(rate_grad)
    gate_grad = gate_grad.astype(jnp.bfloat16)
    up_act_grad = up_act_grad.astype(jnp.bfloat16)
    back_part = lax.dot_general(
        gate_grad, gate_local, (((1,), (1,)), ((), ())), preferred_element_type=jnp.float32
    )
    back_part = back_part + lax.dot_general(
        up_act_grad, up_local, (((1,), (1,)), ((), ())), preferred_element_type=jnp.float32
    )
    route_back = from_experts(back_part.reshape(-1, capacity, model_width), experts, capacity)
    norm_grad = (
        jnp.dot(
            pick_both.T.astype(jnp.float32),
            route_back,
            precision=lax.Precision.HIGHEST,
            preferred_element_type=jnp.float32,
        )
        * gain_row
    )
    section_back = (
        upstream
        + inv_rms * norm_grad
        - tokens
        * (inv_rms * inv_rms * inv_rms)
        * jnp.mean(tokens * norm_grad, axis=-1, keepdims=True)
    )
    passed_back = passed_along(section_back.astype(jnp.bfloat16)[None], "section", -1)
    up_term = lax.dot_general(
        arrived, up_act_grad, (((0,), (0,)), ((), ())), preferred_element_type=jnp.float32
    )
    up_term = up_term.astype(jnp.bfloat16).astype(jnp.float32)
    up_grad = lax.psum_scatter(up_term.astype(jnp.bfloat16), "dp", scatter_dimension=0, tiled=True)[
        None
    ]
    return (passed_on, passed_back, up_grad)


def solution(mesh):
    return jax.shard_map(
        per_device,
        mesh=mesh,
        in_specs=(
            P("section", ("dp", "expert"), None),
            P("section", None),
            P("section", ("dp", "expert"), None),
            P("section", ("dp", "expert"), None),
            P("section", None, "expert"),
            P("section", None, "expert"),
            P("section", "expert"),
            P("section", "expert", "dp"),
            P("section", ("dp", "expert"), None),
        ),
        out_specs=(
            P("section", ("dp", "expert"), None),
            P("section", ("dp", "expert"), None),
            P("section", "dp", "expert"),
        ),
        check_vma=False,
    )
```

profile of v0, /device:TPU:32, one launch (start us, length us, event | category | flops | bytes accessed | tf_op | source)
XLA Modules:
  0.0 712.6 jit_solution(17626897167263078738)
XLA Ops:
  19.0 5.3 broadcast_in_dim.46
  24.4 9.0 %all-to-all-start = ((bf16[32,18,4096]{2,1,0:T(8,128)(2,1)}), bf16[32,18,4096]{2,1,0:T(8,128)(2,1)}, u32[]{:S(2)}, u32[]{:S(2)}) async-start(bf16[32,18,4096]{2,1,0:T(8,128)(2,1)} %bitcast.85), calls=%async_computation | async-start | bytes 12582912 | tf_op jit(solution)/shard_map/all_to_all | solution.py:35
  42.2 126.5 %all-to-all-done = bf16[32,18,4096]{2,1,0:T(8,128)(2,1)} async-done(((bf16[32,18,4096]{2,1,0:T(8,128)(2,1)}), bf16[32,18,4096]{2,1,0:T(8,128)(2,1)}, u32[]{:S(2)}, u32[]{:S(2)}) %all-to-all-start) | async-done | bytes 4718624 | tf_op jit(solution)/shard_map/all_to_all | solution.py:35
  168.7 5.3 broadcast_in_dim.48
  174.0 9.9 %all-to-all-start.2 = ((bf16[32,18,4096]{2,1,0:T(8,128)(2,1)}), bf16[32,18,4096]{2,1,0:T(8,128)(2,1)}, u32[]{:S(2)}, u32[]{:S(2)}) async-start(bf16[32,18,4096]{2,1,0:T(8,128)(2,1)} %bitcast.84), calls=%async_computation.2 | async-start | bytes 12582912 | tf_op jit(solution)/shard_map/all_to_all | solution.py:35
  184.7 7.7 %reshape.97 = bf16[576,4096]{1,0:T(8,128)(2,1)} reshape(bf16[32,18,4096]{2,1,0:T(8,128)(2,1)} %all-to-all-done) | data formatting | bytes 9437184 | tf_op jit(solution)/shard_map/reshape | solution.py:36
  192.4 7.0 fusion.7
  202.9 26.0 %all-gather.3.cloned.1.call-done = bf16[1,384,4096]{2,1,0:T(8,128)(2,1)} async-done(((bf16[1,384,1024]{2,1,0:T(8,128)(2,1)}), bf16[1,384,4096]{2,1,0:T(8,128)(2,1)}) %all-gather.3.cloned.1.call-update) | async-done | bytes 3145744 | tf_op jit(solution)/shard_map/all_gather | solution.py:83
  229.0 9.4 %convolution_convert_fusion = bf16[576,4096]{1,0:T(8,128)(2,1)} fusion(bf16[1,384,4096]{2,1,0:T(8,128)(2,1)} %all-gather.3.cloned.1.call-done, f32[384]{0:T(512)S(1)} %reduce.5, f32[384]{0:T(512)S(1)} %broadcast_multiply_fusion, f32[576,384]{1,0:T(8,128)} %fusion.7, f32[576,384]{1,0:T(8,128)} %fusion.11), kind=kOutput, calls=%fused_computation.3 | convolution fusion | flops 1830002688 | bytes 9636864 | tf_op jit(solution)/shard_map/dot_general | solution.py:87
  238.4 7.6 %convert_element_type.93 = bf16[32,18,4096]{2,1,0:T(8,128)(2,1)} reshape(bf16[576,4096]{1,0:T(8,128)(2,1)} %convolution_convert_fusion) | data formatting | bytes 9437184 | tf_op jit(solution)/shard_map/convert_element_type | solution.py:42
  246.0 73.2 %all-to-all-done.2 = bf16[32,18,4096]{2,1,0:T(8,128)(2,1)} async-done(((bf16[32,18,4096]{2,1,0:T(8,128)(2,1)}), bf16[32,18,4096]{2,1,0:T(8,128)(2,1)}, u32[]{:S(2)}, u32[]{:S(2)}) %all-to-all-start.2) | async-done | bytes 4718624 | tf_op jit(solution)/shard_map/all_to_all | solution.py:35
  319.3 10.2 %all-to-all-start.1 = ((bf16[32,18,4096]{2,1,0:T(8,128)(2,1)}), bf16[32,18,4096]{2,1,0:T(8,128)(2,1)}, u32[]{:S(2)}, u32[]{:S(2)}) async-start(bf16[32,18,4096]{2,1,0:T(8,128)(2,1)} %convert_element_type.93), calls=%async_computation.1 | async-start | bytes 12582912 | tf_op jit(solution)/shard_map/all_to_all | solution.py:41
  329.5 7.7 %reshape.102 = bf16[576,4096]{1,0:T(8,128)(2,1)} reshape(bf16[32,18,4096]{2,1,0:T(8,128)(2,1)} %all-to-all-done.2) | data formatting | bytes 9437184 | tf_op jit(solution)/shard_map/reshape | solution.py:36
  337.3 10.1 %multiply_convert_fusion = (bf16[576,384]{1,0:T(8,128)(2,1)S(1)}, f32[576,384]{1,0:T(8,128)S(1)}) fusion(f32[576,384]{1,0:T(8,128)} %fusion.11, f32[576,384]{1,0:T(8,128)} %fusion.7, f32[384]{0:T(512)S(1)} %broadcast_multiply_fusion, f32[384]{0:T(512)S(1)} %reduce.5, bf16[576,4096]{1,0:T(8,128)(2,1)} %reshape.102, ...), kind=kOutput, calls=%fused_computation.87 | convolution fusion | flops 1840693248 | bytes 10963968 | tf_op jit(solution)/shard_map/dot_general | solution.py:108
  354.5 7.6 %convert_element_type.105 = bf16[32,18,4096]{2,1,0:T(8,128)(2,1)} reshape(bf16[576,4096]{1,0:T(8,128)(2,1)} %add_convert_fusion) | data formatting | bytes 9437184 | tf_op jit(solution)/shard_map/convert_element_type | solution.py:42
  362.1 102.6 %all-to-all-done.1 = bf16[32,18,4096]{2,1,0:T(8,128)(2,1)} async-done(((bf16[32,18,4096]{2,1,0:T(8,128)(2,1)}), bf16[32,18,4096]{2,1,0:T(8,128)(2,1)}, u32[]{:S(2)}, u32[]{:S(2)}) %all-to-all-start.1) | async-done | bytes 4718624 | tf_op jit(solution)/shard_map/all_to_all | solution.py:41
  464.7 9.9 %all-to-all-start.3 = ((bf16[32,18,4096]{2,1,0:T(8,128)(2,1)}), bf16[32,18,4096]{2,1,0:T(8,128)(2,1)}, u32[]{:S(2)}, u32[]{:S(2)}) async-start(bf16[32,18,4096]{2,1,0:T(8,128)(2,1)} %convert_element_type.105), calls=%async_computation.3 | async-start | bytes 12582912 | tf_op jit(solution)/shard_map/all_to_all | solution.py:41
  474.9 7.4 %convolution_convert_fusion.1 = bf16[4096,384]{1,0:T(8,128)(2,1)} fusion(bf16[576,4096]{1,0:T(8,128)(2,1)} %reshape.97, bf16[576,384]{1,0:T(8,128)(2,1)} %copy-done.8), kind=kOutput, calls=%fused_computation.4 | convolution fusion | flops 1813512192 | bytes 8306688 | tf_op jit(solution)/shard_map/dot_general | solution.py:141
  482.2 6.8 bitcast_reduce_fusion.1
  493.4 5.2 fusion.2
  498.6 7.7 %collective-permute-start = (bf16[1,128,4096]{2,1,0:T(8,128)(2,1)}, bf16[1,128,4096]{2,1,0:T(8,128)(2,1)}, u32[]{:S(2)}, u32[]{:S(2)}) collective-permute-start(bf16[1,128,4096]{2,1,0:T(8,128)(2,1)} %fusion.2), channel_id=1, source_target_pairs={{0,128},{1,129},{2,130},{3,131},{4,132},{5,133},{6,134},{7,135},{8... | collective-permute-start | bytes 3145736 | tf_op jit(solution)/shard_map/ppermute | solution.py:17
  506.4 126.0 %all-to-all-done.3 = bf16[32,18,4096]{2,1,0:T(8,128)(2,1)} async-done(((bf16[32,18,4096]{2,1,0:T(8,128)(2,1)}), bf16[32,18,4096]{2,1,0:T(8,128)(2,1)}, u32[]{:S(2)}, u32[]{:S(2)}) %all-to-all-start.3) | async-done | bytes 4718624 | tf_op jit(solution)/shard_map/all_to_all | solution.py:41
  632.4 6.9 bitcast_reduce_fusion
  648.7 52.2 %collective-permute-done.1 = bf16[1,128,4096]{2,1,0:T(8,128)(2,1)} collective-permute-done((bf16[1,128,4096]{2,1,0:T(8,128)(2,1)S(1)}, bf16[1,128,4096]{2,1,0:T(8,128)(2,1)}, u32[]{:S(2)}, u32[]{:S(2)}) %collective-permute-start.1) | collective-permute-done | bytes 1048608 | tf_op jit(solution)/shard_map/ppermute | solution.py:17
  (63 shorter events, 50.6 us)
Async XLA Ops:
  7.2 192.2 %copy-start = (bf16[1,4096,384]{2,1,0:T(8,128)(2,1)S(1)}, bf16[1,4096,384]{2,1,0:T(8,128)(2,1)}, u32[]{:S(2)}) copy-start(bf16[1,4096,384]{2,1,0:T(8,128)(2,1)} %param.13) | copy-start | bytes 9437188
  24.4 9.0 %copy-start.11 = (f32[1,128,2]{1,2,0:T(2,128)S(1)}, f32[1,128,2]{1,2,0:T(2,128)}, u32[]{:S(2)}) copy-start(f32[1,128,2]{1,2,0:T(2,128)} %param.12) | copy-start | bytes 3076
  24.4 144.3 %all-to-all-start = ((bf16[32,18,4096]{2,1,0:T(8,128)(2,1)}), bf16[32,18,4096]{2,1,0:T(8,128)(2,1)}, u32[]{:S(2)}, u32[]{:S(2)}) async-start(bf16[32,18,4096]{2,1,0:T(8,128)(2,1)} %bitcast.85), calls=%async_computation | async-start | bytes 12582912 | tf_op jit(solution)/shard_map/all_to_all | solution.py:35
  33.4 2.2 copy-start.2
  174.0 10.7 %copy-start.10 = (f32[1,384]{1,0:T(1,128)S(1)}, f32[1,384]{1,0:T(1,128)}, u32[]{:S(2)}) copy-start(f32[1,384]{1,0:T(1,128)} %param.15) | copy-start | bytes 4612
  174.0 145.3 %all-to-all-start.2 = ((bf16[32,18,4096]{2,1,0:T(8,128)(2,1)}), bf16[32,18,4096]{2,1,0:T(8,128)(2,1)}, u32[]{:S(2)}, u32[]{:S(2)}) async-start(bf16[32,18,4096]{2,1,0:T(8,128)(2,1)} %bitcast.84), calls=%async_computation.2 | async-start | bytes 12582912 | tf_op jit(solution)/shard_map/all_to_all | solution.py:35
  183.9 45.0 %all-gather.3.cloned.1.call-start = ((), (), s32[]{:S(2)}) async-start(), calls=%async_computation.6 | async-start | bytes 3932160 | tf_op jit(solution)/shard_map/all_gather | solution.py:83
  192.4 7.0 copy-start.4
  319.3 145.4 %all-to-all-start.1 = ((bf16[32,18,4096]{2,1,0:T(8,128)(2,1)}), bf16[32,18,4096]{2,1,0:T(8,128)(2,1)}, u32[]{:S(2)}, u32[]{:S(2)}) async-start(bf16[32,18,4096]{2,1,0:T(8,128)(2,1)} %convert_element_type.93), calls=%async_computation.1 | async-start | bytes 12582912 | tf_op jit(solution)/shard_map/all_to_all | solution.py:41
  337.3 10.1 %copy-start.6 = (f32[576,384]{1,0:T(8,128)S(1)}, f32[576,384]{1,0:T(8,128)}, u32[]{:S(2)}) copy-start(f32[576,384]{1,0:T(8,128)} %fusion.7) | copy-start | bytes 2654212
  337.3 10.2 %copy-start.7 = (f32[576,384]{1,0:T(8,128)S(1)}, f32[576,384]{1,0:T(8,128)}, u32[]{:S(2)}) copy-start(f32[576,384]{1,0:T(8,128)} %fusion.11) | copy-start | bytes 2654212
  347.4 2.8 copy-start.8
  347.4 2.7 copy-start.5
  464.7 167.7 %all-to-all-start.3 = ((bf16[32,18,4096]{2,1,0:T(8,128)(2,1)}), bf16[32,18,4096]{2,1,0:T(8,128)(2,1)}, u32[]{:S(2)}, u32[]{:S(2)}) async-start(bf16[32,18,4096]{2,1,0:T(8,128)(2,1)} %convert_element_type.105), calls=%async_computation.3 | async-start | bytes 12582912 | tf_op jit(solution)/shard_map/all_to_all | solution.py:41
  474.6 226.3 %reduce-scatter.2.cloned.1.call-start = ((), (), s32[]{:S(2)}) async-start(), calls=%async_computation.5 | async-start | bytes 3932160 | tf_op jit(solution)/shard_map/reduce_scatter | solution.py:145
  498.6 150.1 %collective-permute-start = (bf16[1,128,4096]{2,1,0:T(8,128)(2,1)}, bf16[1,128,4096]{2,1,0:T(8,128)(2,1)}, u32[]{:S(2)}, u32[]{:S(2)}) collective-permute-start(bf16[1,128,4096]{2,1,0:T(8,128)(2,1)} %fusion.2), channel_id=1, source_target_pairs={{0,128},{1,129},{2,130},{3,131},{4,132},{5,133},{6,134},{7,135},{8... | collective-permute-start | bytes 3145736 | tf_op jit(solution)/shard_map/ppermute | solution.py:17
  639.3 4.3 copy-start.9
  643.6 3.0 copy-start.1
  643.6 3.0 copy-start.3
  647.4 53.5 %collective-permute-start.1 = (bf16[1,128,4096]{2,1,0:T(8,128)(2,1)S(1)}, bf16[1,128,4096]{2,1,0:T(8,128)(2,1)}, u32[]{:S(2)}, u32[]{:S(2)}) collective-permute-start(bf16[1,128,4096]{2,1,0:T(8,128)(2,1)S(1)} %fusion.26), channel_id=1, source_target_pairs={{128,0},{129,1},{130,2},{131,3},{132,4},{133,5},{134,6},{135,7},{1... | collective-permute-start | bytes 3145736 | tf_op jit(solution)/shard_map/ppermute | solution.py:17
Sparse Core Ops, SparseCore 0:
  186.6 42.3 all-gather.2
  482.3 41.0 reduce-scatter.1
where the time goes:
time: 719 us; the launch traced here: 713 us
  waiting for transfers between devices  507 us (71%)
  local copies, waits for them, and re-layouts  65 us (9%)
  matrix products  60.6 us (8%)
  starting transfers between devices  48.9 us (7%)
  other arithmetic  16.8 us (2%)
  between operations  14.5 us (2%)
    all_to_all x2, waiting for transfers between devices, from_experts(): lax.all_to_all(partials.astype(jnp.bfloat16), 'expert', split_axis=0, con...  229 us
    all_to_all x2, waiting for transfers between devices, to_experts(): lax.all_to_all(doubled, 'expert', split_axis=0, concat_axis=0, tiled=True)  200 us
    ppermute x2, waiting for transfers between devices, passed_along(): lax.ppermute(value, axis, [(source, source + steps) for source in range(l...  52.2 us
    all_gather x1, waiting for transfers between devices, per_device(): down_full = lax.all_gather(down_weight[0], 'dp', axis=1, tiled=True)  26 us
    all_to_all x2, starting transfers between devices, from_experts(): lax.all_to_all(partials.astype(jnp.bfloat16), 'expert', split_axis=0, con...  20.1 us
    all_to_all x2, starting transfers between devices, to_experts(): lax.all_to_all(doubled, 'expert', split_axis=0, concat_axis=0, tiled=True)  18.9 us
    reshape x2, local copies, waits for them, and re-layouts, to_experts(): return gathered.reshape(-1, model_width)  15.5 us
    convert_element_type x2, local copies, waits for them, and re-layouts, from_experts(): partials.astype(jnp.bfloat16)  15.2 us
  transfers between devices with their start and end apart: 8, of which 6 were waited for; matrix products, arithmetic and copies ran while one was open for 16% of the time, Pallas kernels for 0%

commit v1 on v0

v1 whole, which is shorter than its diff:
```python
import functools

import jax
import jax.numpy as jnp
from jax import lax
from jax.experimental import pallas as pl
from jax.experimental.pallas import tpu as pltpu
from jax.sharding import PartitionSpec as P

MESH = pl.DeviceIdType.MESH
TSTEPS = 4
EPS = 1e-06
THETA = 0.5
SHARP = 4.0
HEAD = 16
TAIL = 2
FOLDS = 8
EXPERTS = 16
F32 = jnp.float32
BF16 = jnp.bfloat16


def iota(shape, dim):
    return lax.broadcasted_iota(jnp.int32, shape, dim)


def dot(a, b):
    return jnp.dot(a, b, preferred_element_type=F32)


def dot_t(a, b):
    return lax.dot_general(a, b, (((1,), (1,)), ((), ())), preferred_element_type=F32)


def t_dot(a, b):
    return lax.dot_general(a, b, (((0,), (0,)), ((), ())), preferred_element_type=F32)


def kernel(
    act_ref, cot_ref, gain_ref, ids_ref, gates_ref, leak_ref, gate_hbm, up_hbm, down_hbm,
    res_ref, upgrad_ref,
    gate_w, up_w, down_w, leak_w,
    send_x, send_xe, send_c, send_ce,
    x_rows, x_ext, c_rows, c_ext,
    gate_act, up_act, rate, der_gate, der_up,
    out_rows, out_ext, back_rows, back_ext,
    total, final,
    own_term, sib_term, sib_recv, rep_recv,
    gg, ug,
    w_own_sem, w_sib_send, w_sib_recv, d_send, d_recv, df_send, df_recv,
    x_send, x_recv, c_send, c_recv, local_sem, b_send, b_recv,
    s_send, s_recv, t_send, t_recv, r_send, r_recv,
):
    sec = lax.axis_index("section")
    dp = lax.axis_index("dp")
    lane = lax.axis_index("expert")
    n_dp = lax.axis_size("dp")
    chip = lane // 2
    core = lane % 2
    tokens, width = act_ref.shape
    fold = width // FOLDS
    rows = EXPERTS * HEAD
    slots = rows + EXPERTS * TAIL
    hidden = gate_hbm.shape[1]
    shard = down_hbm.shape[1]

    def peer(step):
        return (sec, dp, lax.rem(chip + step, EXPERTS) * 2 + core)

    sibling = (sec, dp, chip * 2 + (1 - core))
    across = (1 - sec, dp, lane)

    def replica(step):
        return (sec, lax.rem(dp + step, n_dp), lane)

    def remote(src, dst, send, recv, target):
        return pltpu.make_async_remote_copy(
            src_ref=src, dst_ref=dst, send_sem=send, recv_sem=recv,
            device_id=target, device_id_type=MESH,
        )

    barrier = pltpu.get_barrier_semaphore()

    def greet(step, carry):
        pl.semaphore_signal(barrier, inc=1, device_id=peer(step), device_id_type=MESH)
        return carry

    lax.fori_loop(1, EXPERTS, greet, 0)
    for step in range(1, n_dp):
        pl.semaphore_signal(barrier, inc=1, device_id=replica(step), device_id_type=MESH)
    pl.semaphore_signal(barrier, inc=1, device_id=sibling, device_id_type=MESH)
    pl.semaphore_signal(barrier, inc=1, device_id=across, device_id_type=MESH)
    pl.semaphore_wait(barrier, EXPERTS - 1 + n_dp - 1 + 2)

    own_weights = [
        pltpu.make_async_copy(gate_hbm, gate_w.at[core], w_own_sem.at[0]),
        pltpu.make_async_copy(up_hbm, up_w.at[core], w_own_sem.at[1]),
        pltpu.make_async_copy(down_hbm, down_w.at[core, dp], w_own_sem.at[2]),
        pltpu.make_async_copy(leak_ref, leak_w.at[core], w_own_sem.at[3]),
    ]

    def sib_weights(half):
        return [
            remote(gate_hbm, gate_w.at[half], w_sib_send.at[0], w_sib_recv.at[0], sibling),
            remote(up_hbm, up_w.at[half], w_sib_send.at[1], w_sib_recv.at[1], sibling),
            remote(down_hbm, down_w.at[half, dp], w_sib_send.at[2], w_sib_recv.at[2], sibling),
            remote(leak_ref, leak_w.at[half], w_sib_send.at[3], w_sib_recv.at[3], sibling),
        ]

    for copy in own_weights:
        copy.start()
    for copy in sib_weights(core):
        copy.start()

    def down_copy(step, owner):
        return remote(
            down_hbm, down_w.at[core, owner], d_send.at[step - 1], d_recv.at[step - 1], replica(step)
        )

    for step in range(1, n_dp):
        down_copy(step, dp).start()

    ids = ids_ref[...]
    gates = gates_ref[...]
    named = iota((EXPERTS, tokens), 0)
    first = jnp.where(ids[0:1, :] == named, 1.0, 0.0).astype(F32)
    second = jnp.where(ids[1:2, :] == named, 1.0, 0.0).astype(F32)
    both = first + second
    earlier = jnp.where(iota((tokens, tokens), 0) < iota((tokens, tokens), 1), 1.0, 0.0)
    counts = dot(both.astype(BF16), earlier.astype(BF16))
    gate_of = first * gates[0:1, :] + second * gates[1:2, :]
    spread = jnp.where(iota((rows, EXPERTS), 0) // HEAD == iota((rows, EXPERTS), 1), 1.0, 0.0)
    spread16 = spread.astype(BF16)
    both_x = dot(spread16, both.astype(BF16))
    counts_x = dot(spread16, counts.astype(BF16))
    gate_x = jnp.dot(spread, gate_of, precision=lax.Precision.HIGHEST, preferred_element_type=F32)
    row_at = iota((rows, tokens), 0)
    head = both_x * jnp.where(counts_x == (row_at % HEAD).astype(F32), 1.0, 0.0)
    tail = both_x * jnp.where(counts_x == (HEAD + row_at % TAIL).astype(F32), 1.0, 0.0)
    fold_at = (row_at % HEAD) // TAIL
    head_gate = jnp.sum(head * gate_x, axis=1, keepdims=True)
    tail_gate = jnp.sum(tail * gate_x, axis=1, keepdims=True)
    head16 = head.astype(BF16)

    acts = act_ref[...].astype(F32)
    inv_rms = lax.rsqrt(jnp.mean(acts * acts, axis=-1, keepdims=True) + EPS)

    def columns(at):
        return pl.ds(pl.multiple_of(at * fold, fold), fold)

    def prepare(at, carry):
        cols = columns(at)
        normed = (act_ref[:, cols].astype(F32) * inv_rms * gain_ref[:, cols]).astype(BF16)
        send_x[:, cols] = dot(head16, normed).astype(BF16)
        part = jnp.where(fold_at == at, tail, 0.0).astype(BF16)
        return carry + dot(part, normed)

    ext = lax.fori_loop(0, FOLDS, prepare, jnp.zeros((rows, fold), F32))
    send_xe[...] = ext.astype(BF16)

    def block(at):
        return pl.ds(pl.multiple_of(at * HEAD, HEAD), HEAD)

    def exchange(src, dst, ext_src, ext_dst, send, recv, step, there, landed):
        return (
            remote(src.at[block(there), :], dst.at[block(landed), :], send.at[step], recv.at[step], peer(step)),
            remote(
                ext_src.at[block(there), :], ext_dst.at[block(landed), :],
                send.at[EXPERTS + step], recv.at[EXPERTS + step], peer(step),
            ),
        )

    def send_all(src, dst, ext_src, ext_dst, send, recv):
        def body(step, carry):
            there = lax.rem(chip + step, EXPERTS)
            for copy in exchange(src, dst, ext_src, ext_dst, send, recv, step, there, chip):
                copy.start()
            return carry

        lax.fori_loop(1, EXPERTS, body, 0)

    def wait_all(src, dst, ext_src, ext_dst, send, recv):
        def body(step, carry):
            origin = lax.rem(chip + EXPERTS - step, EXPERTS)
            for copy in exchange(src, dst, ext_src, ext_dst, send, recv, step, origin, origin):
                copy.wait_recv()
            return carry

        lax.fori_loop(1, EXPERTS, body, 0)

    def wait_sent(src, dst, ext_src, ext_dst, send, recv):
        def body(step, carry):
            there = lax.rem(chip + step, EXPERTS)
            for copy in exchange(src, dst, ext_src, ext_dst, send, recv, step, there, chip):
                copy.wait_send()
            return carry

        lax.fori_loop(1, EXPERTS, body, 0)

    def keep_own(src, dst, ext_src, ext_dst):
        dst[block(chip), :] = src[block(chip), :]
        ext_dst[block(chip), :] = ext_src[block(chip), :]

    x_way = (send_x, x_rows, send_xe, x_ext)
    c_way = (send_c, c_rows, send_ce, c_ext)
    b_way = (out_rows, back_rows, out_ext, back_ext)
    send_all(*x_way, x_send, x_recv)
    keep_own(*x_way)

    def prepare_grad(at, carry):
        cols = columns(at)
        upstream = cot_ref[:, cols]
        send_c[:, cols] = (dot(head16, upstream) * head_gate).astype(BF16)
        part = jnp.where(fold_at == at, tail, 0.0).astype(BF16)
        return carry + dot(part, upstream)

    ext = lax.fori_loop(0, FOLDS, prepare_grad, jnp.zeros((rows, fold), F32))
    send_ce[...] = (ext * tail_gate).astype(BF16)
    send_all(*c_way, c_send, c_recv)
    keep_own(*c_way)

    for copy in own_weights:
        copy.wait()
    for copy in sib_weights(1 - core):
        copy.wait_recv()
    for copy in sib_weights(core):
        copy.wait_send()

    def forward_down(step, half, owner):
        return remote(
            down_w.at[core, owner], down_w.at[half, owner],
            df_send.at[step - 1], df_recv.at[step - 1], sibling,
        )

    for step in range(1, n_dp):
        owner = lax.rem(dp + n_dp - step, n_dp)
        down_copy(step, owner).wait_recv()
        forward_down(step, core, owner).start()
    for step in range(1, n_dp):
        owner = lax.rem(dp + n_dp - step, n_dp)
        forward_down(step, 1 - core, owner).wait_recv()
        forward_down(step, core, owner).wait_send()
        down_copy(step, dp).wait_send()

    unfold_row = iota((EXPERTS * TAIL, rows), 0)
    unfold_col = iota((EXPERTS * TAIL, rows), 1)
    same = jnp.logical_and(
        unfold_row // TAIL == unfold_col // HEAD, unfold_row % TAIL == unfold_col % TAIL
    )
    unfold = jnp.where(same, 1.0, 0.0)
    unfold_at = (unfold_col % HEAD) // TAIL
    refold_row = iota((rows, EXPERTS * TAIL), 0)
    refold_col = iota((rows, EXPERTS * TAIL), 1)
    alike = jnp.logical_and(
        refold_col // TAIL == refold_row // HEAD, refold_col % TAIL == refold_row % TAIL
    )
    refold = jnp.where(alike, 1.0, 0.0)
    refold_at = (refold_row % HEAD) // TAIL

    def unfold_tail(ext_ref, rows_ref):
        def body(at, carry):
            pick = jnp.where(unfold_at == at, unfold, 0.0).astype(BF16)
            rows_ref[rows:slots, columns(at)] = dot(pick, ext_ref[...]).astype(BF16)
            return carry

        lax.fori_loop(0, FOLDS, body, 0)

    wait_all(*x_way, x_send, x_recv)
    unfold_tail(x_ext, x_rows)

    for half in range(2):
        gate_act[half] = jnp.zeros((slots, hidden), F32)
        up_act[half] = jnp.zeros((slots, hidden), F32)

        def project(at, carry):
            cols = columns(at)
            gate_act[half] += dot(x_rows[:, cols], gate_w[half, cols, :])
            up_act[half] += dot(x_rows[:, cols], up_w[half, cols, :])
            return carry

        lax.fori_loop(0, FOLDS, project, 0)

        def spiking(at, carry):
            part = pl.ds(pl.multiple_of(at * 32, 32), 32)
            gate_in = gate_act[half, part, :]
            up_in = up_act[half, part, :]
            leak = leak_w[half, 0:1, :]
            opened = lax.logistic(gate_in)
            silu = gate_in * opened
            drive = silu * up_in
            volts = drive
            volts_d = jnp.ones_like(drive)
            spike_sum = jnp.zeros_like(drive)
            spike_d = jnp.zeros_like(drive)
            for timestep in range(TSTEPS):
                if timestep:
                    volts = leak * volts + drive
                    volts_d = leak * volts_d + 1.0
                plus = lax.logistic(SHARP * (volts - THETA))
                minus = lax.logistic(SHARP * (-volts - THETA))
                spikes = plus - minus
                slope = SHARP * (plus * (1.0 - plus) + minus * (1.0 - minus))
                spikes_d = slope * volts_d
                volts = volts - THETA * spikes
                volts_d = volts_d - THETA * spikes_d
                spike_sum = spike_sum + spikes
                spike_d = spike_d + spikes_d
            rate[half, part, :] = (spike_sum / TSTEPS).astype(BF16)
            drive_d = spike_d / TSTEPS
            der_gate[half, part, :] = drive_d * up_in * (opened * (1.0 + gate_in * (1.0 - opened)))
            der_up[half, part, :] = drive_d * silu
            return carry

        lax.fori_loop(0, slots // 32, spiking, 0)

    def fold_tail():
        def body(at, carry):
            pick = jnp.where(refold_at == at, refold, 0.0).astype(BF16)
            return carry + dot(pick, out_rows[rows:slots, columns(at)])

        out_ext[...] = lax.fori_loop(0, FOLDS, body, jnp.zeros((rows, fold), F32)).astype(BF16)

    @pl.when(sec == 0)
    def _():
        for owner in range(n_dp):
            out_rows[:, owner * shard : (owner + 1) * shard] = (
                dot(rate[0], down_w[0, owner]) + dot(rate[1], down_w[1, owner])
            ).astype(BF16)
        fold_tail()
        send_all(*b_way, b_send, b_recv)
        keep_own(*b_way)

    wait_all(*c_way, c_send, c_recv)
    unfold_tail(c_ext, c_rows)
    for half in range(2):
        rate_grad = jnp.zeros((slots, hidden), F32)
        for owner in range(n_dp):
            rate_grad = rate_grad + dot_t(
                c_rows[:, owner * shard : (owner + 1) * shard], down_w[half, owner]
            )
        gg[half] = (rate_grad * der_gate[half]).astype(BF16)
        ug[half] = (rate_grad * der_up[half]).astype(BF16)

    @pl.when(sec == 1)
    def _():
        def body(at, carry):
            cols = columns(at)
            out_rows[:, cols] = (
                dot_t(gg[0], gate_w[0, cols, :]) + dot_t(gg[1], gate_w[1, cols, :])
                + dot_t(ug[0], up_w[0, cols, :]) + dot_t(ug[1], up_w[1, cols, :])
            ).astype(BF16)
            return carry

        lax.fori_loop(0, FOLDS, body, 0)
        fold_tail()
        send_all(*b_way, b_send, b_recv)
        keep_own(*b_way)

    def sib_copy(step, at):
        part = pl.ds(pl.multiple_of(at * shard, shard), shard)
        return remote(sib_term.at[part, :], sib_recv.at[part, :], t_send.at[step], t_recv.at[step], sibling)

    def rep_copy(step, at):
        part = pl.ds(pl.multiple_of(at * shard, shard), shard)
        return remote(
            sib_recv.at[part, :], rep_recv.at[step - 1], r_send.at[step - 1], r_recv.at[step - 1], replica(step)
        )

    halves = shard // 2
    for step in range(n_dp + 1):
        if step < n_dp:
            at = lax.rem(dp + step + 1, n_dp)
            for piece in range(2):
                low = piece * halves
                part = pl.ds(pl.multiple_of(at * shard + low, halves), halves)
                own_term[step % 2, low : low + halves, :] = t_dot(x_rows[:, part], ug[core])
                sib_term[part, :] = t_dot(x_rows[:, part], ug[1 - core]).astype(BF16)
            sib_copy(step, at).start()
        if step > 0:
            at = lax.rem(dp + step, n_dp)
            sib_copy(step - 1, at).wait()
            part = pl.ds(pl.multiple_of(at * shard, shard), shard)
            sib_recv[part, :] = (own_term[(step - 1) % 2] + sib_recv[part, :].astype(F32)).astype(BF16)
            if step < n_dp:
                rep_copy(step, at).start()

    wait_all(*b_way, b_send, b_recv)

    def pass_copy(at):
        return remote(
            final.at[:, columns(at)], res_ref.at[:, columns(at)], s_send.at[at], s_recv.at[at], across
        )

    is_first = sec == 0
    head_mix = jnp.where(is_first, head * gate_x, head).T.astype(BF16)
    tail_mix = jnp.where(is_first, tail * gate_x, tail).T
    fold_t = (iota((tokens, rows), 1) % HEAD) // TAIL

    def mixed(at):
        cols = columns(at)
        part = jnp.where(fold_t == at, tail_mix, 0.0).astype(BF16)
        return dot(head_mix, back_rows[:, cols]) + dot(part, back_ext[...])

    @pl.when(sec == 0)
    def _():
        def body(at, carry):
            cols = columns(at)
            final[:, cols] = (act_ref[:, cols].astype(F32) + mixed(at)).astype(BF16)
            pass_copy(at).start()
            return carry

        lax.fori_loop(0, FOLDS, body, 0)

    @pl.when(sec == 1)
    def _():
        def gather(at, carry):
            cols = columns(at)
            norm_grad = mixed(at) * gain_ref[:, cols]
            total[:, cols] = norm_grad
            return carry + jnp.sum(act_ref[:, cols].astype(F32) * norm_grad, axis=-1, keepdims=True)

        mean = lax.fori_loop(0, FOLDS, gather, jnp.zeros((tokens, 1), F32)) / width
        scale = inv_rms * inv_rms * inv_rms * mean

        def body(at, carry):
            cols = columns(at)
            final[:, cols] = (
                cot_ref[:, cols].astype(F32)
                + inv_rms * total[:, cols]
                - act_ref[:, cols].astype(F32) * scale
            ).astype(BF16)
            pass_copy(at).start()
            return carry

        lax.fori_loop(0, FOLDS, body, 0)

    for step in range(1, n_dp):
        rep_copy(step, dp).wait_recv()
    own = pl.ds(pl.multiple_of(dp * shard, shard), shard)
    total_grad = sib_recv[own, :].astype(F32)
    for step in range(1, n_dp):
        total_grad = total_grad + rep_recv[step - 1].astype(F32)
    upgrad_ref[...] = total_grad.astype(BF16)

    wait_sent(*x_way, x_send, x_recv)
    wait_sent(*c_way, c_send, c_recv)
    wait_sent(*b_way, b_send, b_recv)
    for step in range(1, n_dp):
        rep_copy(step, dp).wait_send()

    def finish(at, carry):
        pass_copy(at).wait()
        return carry

    lax.fori_loop(0, FOLDS, finish, 0)


def per_device(
    activations, norm_gain, route_ids, route_gates, gate_weight, up_weight, leak_rates, down_weight, cotangent
):
    tokens, width = activations.shape[1:]
    hidden = gate_weight.shape[2]
    shard = down_weight.shape[2]
    n_dp = lax.axis_size("dp")
    rows = EXPERTS * HEAD
    slots = rows + EXPERTS * TAIL
    fold = width // FOLDS
    vmem = pl.BlockSpec(memory_space=pltpu.VMEM)
    anywhere = pl.BlockSpec(memory_space=pl.ANY)
    dma = pltpu.SemaphoreType.DMA

    def scratch(kind, *shape):
        return pltpu.VMEM(shape, kind)

    result, up_grad = pl.pallas_call(
        kernel,
        out_shape=(
            jax.ShapeDtypeStruct((tokens, width), BF16),
            jax.ShapeDtypeStruct((shard, hidden), BF16),
        ),
        in_specs=[vmem] * 6 + [anywhere] * 3,
        out_specs=(anywhere, vmem),
        scratch_shapes=[
            scratch(BF16, 2, width, hidden),
            scratch(BF16, 2, width, hidden),
            scratch(BF16, 2, n_dp, hidden, shard),
            scratch(F32, 2, 8, hidden),
            scratch(BF16, rows, width),
            scratch(BF16, rows, fold),
            scratch(BF16, rows, width),
            scratch(BF16, rows, fold),
            scratch(BF16, slots, width),
            scratch(BF16, rows, fold),
            scratch(BF16, slots, width),
            scratch(BF16, rows, fold),
            scratch(F32, 2, slots, hidden),
            scratch(F32, 2, slots, hidden),
            scratch(BF16, 2, slots, hidden),
            scratch(F32, 2, slots, hidden),
            scratch(F32, 2, slots, hidden),
            scratch(BF16, slots, width),
            scratch(BF16, rows, fold),
            scratch(BF16, rows, width),
            scratch(BF16, rows, fold),
            scratch(F32, tokens, width),
            scratch(BF16, tokens, width),
            scratch(F32, 2, shard, hidden),
            scratch(BF16, width, hidden),
            scratch(BF16, width, hidden),
            scratch(BF16, n_dp - 1, shard, hidden),
            scratch(BF16, 2, slots, hidden),
            scratch(BF16, 2, slots, hidden),
            dma((4,)), dma((4,)), dma((4,)),
            dma((n_dp - 1,)), dma((n_dp - 1,)), dma((n_dp - 1,)), dma((n_dp - 1,)),
            dma((2 * EXPERTS,)), dma((2 * EXPERTS,)), dma((2 * EXPERTS,)), dma((2 * EXPERTS,)),
            dma((1,)), dma((2 * EXPERTS,)), dma((2 * EXPERTS,)),
            dma((FOLDS,)), dma((FOLDS,)), dma((n_dp,)), dma((n_dp,)),
            dma((n_dp - 1,)), dma((n_dp - 1,)),
        ],
        compiler_params=pltpu.CompilerParams(
            collective_id=0, has_side_effects=True, vmem_limit_bytes=60 * 2**20
        ),
    )(
        activations[0],
        cotangent[0],
        norm_gain,
        route_ids[0].T,
        route_gates[0].T,
        jnp.broadcast_to(leak_rates, (8, hidden)),
        gate_weight[0],
        up_weight[0],
        down_weight[0],
    )
    first = lax.axis_index("section") == 0
    nothing = jnp.zeros_like(result)
    passed_on = jnp.where(first, nothing, result)
    passed_back = jnp.where(first, result, nothing)
    return (passed_on[None], passed_back[None], up_grad[None])


def solution(mesh):
    return jax.shard_map(
        per_device,
        mesh=mesh,
        in_specs=(
            P("section", ("dp", "expert"), None),
            P("section", None),
            P("section", ("dp", "expert"), None),
            P("section", ("dp", "expert"), None),
            P("section", None, "expert"),
            P("section", None, "expert"),
            P("section", "expert"),
            P("section", "expert", "dp"),
            P("section", ("dp", "expert"), None),
        ),
        out_specs=(
            P("section", ("dp", "expert"), None),
            P("section", ("dp", "expert"), None),
            P("section", "dp", "expert"),
        ),
        check_vma=False,
    )
```

time: 719 us -> 260 us (0.36)
  the two profiles are of different devices: /device:TPU:32 before, /device:TPU:104 now
where the time goes in v1:
time: 260 us
  Pallas kernels  255 us (98%)
  other arithmetic  3.46 us (1%)
    pallas_call x1, Pallas kernels, per_device(): pl.pallas_call(kernel, out_shape=(jax.ShapeDtypeStruct((tokens, width), B...  255 us

profile of v1, /device:TPU:104, one launch (start us, length us, event | category | flops | bytes accessed | tf_op | source)
XLA Modules:
  0.0 260.3 jit_solution(5244264568335923462)
XLA Ops:
  0.6 0.7 reduce
  1.3 0.6 broadcast_in_dim.21.leak_ref
  1.9 254.7 %shard_map.112 = (bf16[128,4096]{1,0:T(8,128)(2,1)}, bf16[1024,384]{1,0:T(8,128)(2,1)}) custom-call(bf16[128,4096]{1,0:T(8,128)(2,1)} %bitcast.18, bf16[128,4096]{1,0:T(8,128)(2,1)} %bitcast.19, f32[1,4096]{1,0:T(1,128)} %gain_ref.1, s32[2,128]{1,0:T(2,128)} %bitcast.22, f32[2,128]{1,0:T(2,128)} %bitcast.23, f32[8,384]{1,0:T(8,128)} %broadcast_in_dim.21.leak_ref, ...), custom_call_target="tpu_custom_call" | custom-call | tf_op jit(solution)/shard_map/pallas_call | solution.py:475
  256.6 0.0 copy-start
  256.6 2.8 %select_bitcast_fusion = (bf16[1,128,4096]{2,1,0:T(8,128)(2,1)}, bf16[1,128,4096]{2,1,0:T(8,128)(2,1)}) fusion(bf16[128,4096]{1,0:T(8,128)(2,1)} %get-tuple-element.5, pred[]{:T(512)S(6)} %eq.3), kind=kLoop, calls=%fused_computation | loop fusion | flops 1048576 | bytes 3145729 | tf_op jit(solution)/shard_map/broadcast_in_dim | solution.py:538
  259.4 0.0 copy-done
  259.4 0.9 copy.13
Async XLA Ops:
  256.6 2.8 %copy-start = (bf16[1024,384]{1,0:T(8,128)(2,1)S(1)}, bf16[1024,384]{1,0:T(8,128)(2,1)}, u32[]{:S(2)}) copy-start(bf16[1024,384]{1,0:T(8,128)(2,1)} %get-tuple-element.6) | copy-start | bytes 2359300

commit v2 on v1

v2 whole, which is shorter than its diff:
```python
import functools

import jax
import jax.numpy as jnp
from jax import lax
from jax.experimental import pallas as pl
from jax.experimental.pallas import tpu as pltpu
from jax.sharding import PartitionSpec as P

MESH = pl.DeviceIdType.MESH
TSTEPS = 4
EPS = 1e-06
THETA = 0.5
SHARP = 4.0
HEAD = 16
TAIL = 2
FOLDS = 8
LANES = 128
QUARTERS = 4
EXPERTS = 16
RUN = 4
F32 = jnp.float32
BF16 = jnp.bfloat16


def iota(shape, dim):
    return lax.broadcasted_iota(jnp.int32, shape, dim)


def dot(a, b):
    return jnp.dot(a, b, preferred_element_type=F32)


def dot_t(a, b):
    return lax.dot_general(a, b, (((1,), (1,)), ((), ())), preferred_element_type=F32)


def t_dot(a, b):
    return lax.dot_general(a, b, (((0,), (0,)), ((), ())), preferred_element_type=F32)


def folds(value):
    return jnp.concatenate([value[:, at * LANES : (at + 1) * LANES] for at in range(FOLDS)], axis=0)


def fold_order(blocks, inverse):
    size = blocks * HEAD
    by_fold, by_block = iota((size, size), int(inverse)), iota((size, size), 1 - int(inverse))
    match = jnp.logical_and(
        by_fold // (blocks * TAIL) == (by_block % HEAD) // TAIL,
        jnp.logical_and(
            (by_fold % (blocks * TAIL)) // TAIL == by_block // HEAD, by_fold % TAIL == by_block % TAIL
        ),
    )
    return jnp.where(match, 1.0, 0.0).astype(BF16)


def routes(ids, tokens):
    named = iota((EXPERTS, tokens), 0).astype(F32)
    first = jnp.where(ids[0:1, :] == named, 1.0, 0.0)
    second = jnp.where(ids[1:2, :] == named, 1.0, 0.0)
    both = first + second
    earlier = jnp.where(iota((tokens, tokens), 0) < iota((tokens, tokens), 1), 1.0, 0.0)
    counts = dot(both.astype(BF16), earlier.astype(BF16))
    return first, second, both, counts


def slots_of(expert_at, slot_at, both, counts, weights):
    spread = jnp.where(expert_at[:, :EXPERTS] == iota((expert_at.shape[0], EXPERTS), 1), 1.0, 0.0)
    both_x = dot(spread.astype(BF16), both.astype(BF16))
    counts_x = dot(spread.astype(BF16), counts.astype(BF16))
    weights_x = jnp.dot(spread, weights, precision=lax.Precision.HIGHEST, preferred_element_type=F32)
    taken = both_x * jnp.where(counts_x == slot_at.astype(F32), 1.0, 0.0)
    return taken, taken * weights_x


def kernel(
    act_ref, cot_ref, gain_ref, ids_ref, gates_ref, leak_ref, gate_hbm, up_hbm, down_hbm,
    res_ref, upgrad_ref,
    gate_w, up_w, down_w, leak_w,
    send_x, send_xe, send_c, send_ce,
    x_rows, x_ext, c_rows, c_ext,
    gate_act, up_act, rate, der_gate, der_up, rate_grad,
    out_rows, out_ext, back_rows, back_ext, far_rows, far_ext,
    final, landed, meta, meta_recv, dots, dots_recv, mix, far_mix,
    own_term, sib_term, sib_recv, rep_recv,
    gg, ug,
    w_own_sem, w_sib_send, w_sib_recv, d_send, d_recv, df_send, df_recv,
    x_send, x_recv, c_send, c_recv, b_send, b_recv, f_recv,
    s_send, s_recv, t_send, t_recv, r_send, r_recv, m_send, m_recv, v_send, v_recv,
):
    sec = lax.axis_index("section")
    dp = lax.axis_index("dp")
    lane = lax.axis_index("expert")
    n_dp = lax.axis_size("dp")
    chip = lane // 2
    core = lane % 2
    depth = chip % RUN
    tokens, width = act_ref.shape
    quarter = width // QUARTERS
    rows = EXPERTS * HEAD
    slots = rows + EXPERTS * TAIL
    hidden = gate_hbm.shape[1]
    shard = down_hbm.shape[1]
    far_blocks = EXPERTS // 2
    far_heads = far_blocks * HEAD
    far_slots = far_heads + far_blocks * TAIL

    def peer(step, section=sec):
        return (section, dp, lax.rem(chip + step, EXPERTS) * 2 + core)

    sibling = (sec, dp, chip * 2 + (1 - core))
    across = (1 - sec, dp, lane)

    def replica(step):
        return (sec, lax.rem(dp + step, n_dp), lane)

    def at_edge(place):
        return ((place + 1) // 2 + 1) % 2

    def is_far(home, expert):
        home_at, expert_at = home % RUN, expert % RUN
        return at_edge(home_at) * ((home_at // 2 + expert_at // 2) % 2)

    def remote(src, dst, send, recv, target):
        return pltpu.make_async_remote_copy(
            src_ref=src, dst_ref=dst, send_sem=send, recv_sem=recv,
            device_id=target, device_id_type=MESH,
        )

    barrier = pltpu.get_barrier_semaphore()

    def greet(step, carry):
        pl.semaphore_signal(barrier, inc=1, device_id=peer(step), device_id_type=MESH)
        pl.semaphore_signal(barrier, inc=1, device_id=peer(step, 1 - sec), device_id_type=MESH)
        return carry

    lax.fori_loop(1, EXPERTS, greet, 0)
    for step in range(1, n_dp):
        pl.semaphore_signal(barrier, inc=1, device_id=replica(step), device_id_type=MESH)
    pl.semaphore_signal(barrier, inc=1, device_id=sibling, device_id_type=MESH)
    pl.semaphore_signal(barrier, inc=1, device_id=across, device_id_type=MESH)

    ids = ids_ref[...].astype(F32)
    gates = gates_ref[...]
    first, second, both, counts = routes(ids, tokens)
    gate_of = first * gates[0:1, :] + second * gates[1:2, :]
    row_at = iota((slots, tokens), 0)
    in_head = row_at < rows
    expert_at = jnp.where(in_head, row_at // HEAD, (row_at - rows) // TAIL)
    slot_at = jnp.where(in_head, row_at % HEAD, HEAD + row_at % TAIL)
    taken, taken_gate = slots_of(expert_at, slot_at, both, counts, gate_of)
    slot_gate = jnp.sum(taken_gate, axis=1, keepdims=True)
    pick = taken.astype(BF16)
    fold_up = fold_order(EXPERTS, True)
    unfold_all = fold_order(EXPERTS, False)

    acts = act_ref[...].astype(F32)
    inv_rms = lax.rsqrt(jnp.mean(acts * acts, axis=-1, keepdims=True) + EPS)

    def columns(at):
        return slice(at * quarter, (at + 1) * quarter)

    def lanes(at):
        return slice(at * LANES, (at + 1) * LANES)

    def block(at):
        return pl.ds(pl.multiple_of(at * HEAD, HEAD), HEAD)

    def store_slots(at, value, head_ref, ext_ref):
        head_ref[0:rows, columns(at)] = value[0:rows].astype(BF16)
        ext_ref[:, lanes(at)] = dot(fold_up, folds(value[rows:slots].astype(BF16))).astype(BF16)

    def unfold(at, head_ref, ext_ref, order, heads, tails):
        back = dot(order, ext_ref[:, lanes(at)]).astype(BF16)
        for fold in range(FOLDS):
            low = at * quarter + fold * LANES
            head_ref[heads : heads + tails, low : low + LANES] = back[fold * tails : (fold + 1) * tails]

    def pieces(way, sems, at, step, there, landed_at):
        src, dst, ext_src, ext_dst = way
        send, recv = sems
        return (
            remote(
                src.at[block(there), columns(at)], dst.at[block(landed_at), columns(at)],
                send.at[at, step], recv.at[at, step], peer(step),
            ),
            remote(
                ext_src.at[block(there), lanes(at)], ext_dst.at[block(landed_at), lanes(at)],
                send.at[at, EXPERTS + step], recv.at[at, EXPERTS + step], peer(step),
            ),
        )

    def send_all(way, sems, at):
        def body(step, carry):
            for copy in pieces(way, sems, at, step, lax.rem(chip + step, EXPERTS), chip):
                copy.start()
            return carry

        lax.fori_loop(1, EXPERTS, body, 0)

    def wait_all(way, sems, at):
        def body(step, carry):
            origin = lax.rem(chip + EXPERTS - step, EXPERTS)
            for copy in pieces(way, sems, at, step, origin, origin):
                copy.wait_recv()
            return carry

        lax.fori_loop(1, EXPERTS, body, 0)

    def wait_sent(way, sems):
        for at in range(QUARTERS):

            def body(step, carry):
                for copy in pieces(way, sems, at, step, lax.rem(chip + step, EXPERTS), chip):
                    copy.wait_send()
                return carry

            lax.fori_loop(1, EXPERTS, body, 0)

    def keep_own(way, at):
        src, dst, ext_src, ext_dst = way
        dst[block(chip), columns(at)] = src[block(chip), columns(at)]
        ext_dst[block(chip), lanes(at)] = ext_src[block(chip), lanes(at)]

    x_way, x_sems = (send_x, x_rows, send_xe, x_ext), (x_send, x_recv)
    c_way, c_sems = (send_c, c_rows, send_ce, c_ext), (c_send, c_recv)
    b_way, b_sems = (out_rows, back_rows, out_ext, back_ext), (b_send, b_recv)

    own_weights = [
        pltpu.make_async_copy(gate_hbm, gate_w.at[core], w_own_sem.at[0]),
        pltpu.make_async_copy(up_hbm, up_w.at[core], w_own_sem.at[1]),
        pltpu.make_async_copy(down_hbm, down_w.at[core, dp], w_own_sem.at[2]),
        pltpu.make_async_copy(leak_ref, leak_w.at[core], w_own_sem.at[3]),
    ]

    def sib_weights(half):
        return [
            remote(gate_hbm, gate_w.at[half], w_sib_send.at[0], w_sib_recv.at[0], sibling),
            remote(up_hbm, up_w.at[half], w_sib_send.at[1], w_sib_recv.at[1], sibling),
            remote(down_hbm, down_w.at[half, dp], w_sib_send.at[2], w_sib_recv.at[2], sibling),
            remote(leak_ref, leak_w.at[half], w_sib_send.at[3], w_sib_recv.at[3], sibling),
        ]

    def down_copy(step, owner):
        return remote(
            down_hbm, down_w.at[core, owner], d_send.at[step - 1], d_recv.at[step - 1], replica(step)
        )

    def meta_copy():
        return remote(meta, meta_recv, m_send.at[0], m_recv.at[0], across)

    def prepare(at):
        cols = columns(at)
        normed = (act_ref[:, cols].astype(F32) * inv_rms * gain_ref[:, cols]).astype(BF16)
        store_slots(at, dot(pick, normed), send_x, send_xe)

    prepare(0)
    pl.semaphore_wait(barrier, 2 * (EXPERTS - 1) + n_dp - 1 + 2)
    send_all(x_way, x_sems, 0)

    for copy in own_weights:
        copy.start()
    for copy in sib_weights(core):
        copy.start()
    for step in range(1, n_dp):
        down_copy(step, dp).start()

    for at in range(1, QUARTERS):
        prepare(at)
        send_all(x_way, x_sems, at)
    for at in range(QUARTERS):
        store_slots(at, dot(pick, cot_ref[:, columns(at)]) * slot_gate, send_c, send_ce)
        send_all(c_way, c_sems, at)
    for at in range(QUARTERS):
        keep_own(x_way, at)
        keep_own(c_way, at)

    one = jnp.where(iota((tokens, tokens), 0) == iota((tokens, tokens), 1), 1.0, 0.0)
    inv_row = jnp.sum(one * inv_rms, axis=0, keepdims=True)
    is_first = sec == 0
    meta[...] = jnp.zeros_like(meta)
    meta[0:2, :] = ids
    meta[2:3, :] = jnp.where(is_first, gates[0:1, :], inv_row)
    meta[3:4, :] = jnp.where(is_first, gates[1:2, :], inv_row)
    meta_copy().start()

    differs = jnp.where((expert_at % RUN) // 2 == depth // 2, 0.0, 1.0) * at_edge(depth).astype(F32)
    mix[...] = (jnp.where(is_first, taken_gate, taken * inv_row) * (1.0 - differs)).T.astype(BF16)

    def clear(origin, carry):
        @pl.when(is_far(chip, origin) == 1)
        def _():
            back_rows[block(origin), :] = jnp.zeros((HEAD, width), BF16)
            back_ext[block(origin), :] = jnp.zeros((HEAD, QUARTERS * LANES), BF16)

        return carry

    lax.fori_loop(0, EXPERTS, clear, 0)

    for copy in own_weights:
        copy.wait()
    for copy in sib_weights(1 - core):
        copy.wait_recv()
    for copy in sib_weights(core):
        copy.wait_send()

    for at in range(QUARTERS):
        wait_all(x_way, x_sems, at)
        unfold(at, x_rows, x_ext, unfold_all, rows, slots - rows)
        for half in range(2):
            for weight, total in ((gate_w, gate_act), (up_w, up_act)):
                part = dot(x_rows[:, columns(at)], weight[half, columns(at), :])
                total[half] = part if at == 0 else total[half] + part

    for half in range(2):

        def spiking(at, carry):
            part = pl.ds(pl.multiple_of(at * 32, 32), 32)
            gate_in = gate_act[half, part, :]
            up_in = up_act[half, part, :]
            leak = leak_w[half, 0:1, :]
            opened = lax.logistic(gate_in)
            silu = gate_in * opened
            drive = silu * up_in
            volts = drive
            volts_d = jnp.ones_like(drive)
            spike_sum = jnp.zeros_like(drive)
            spike_d = jnp.zeros_like(drive)
            for timestep in range(TSTEPS):
                if timestep:
                    volts = leak * volts + drive
                    volts_d = leak * volts_d + 1.0
                plus = lax.logistic(SHARP * (volts - THETA))
                minus = lax.logistic(SHARP * (-volts - THETA))
                spikes = plus - minus
                slope = SHARP * (plus * (1.0 - plus) + minus * (1.0 - minus))
                spikes_d = slope * volts_d
                volts = volts - THETA * spikes
                volts_d = volts_d - THETA * spikes_d
                spike_sum = spike_sum + spikes
                spike_d = spike_d + spikes_d
            rate[half, part, :] = (spike_sum / TSTEPS).astype(BF16)
            drive_d = spike_d / TSTEPS
            der_gate[half, part, :] = drive_d * up_in * (opened * (1.0 + gate_in * (1.0 - opened)))
            der_up[half, part, :] = drive_d * silu
            return carry

        lax.fori_loop(0, slots // 32, spiking, 0)

    def forward_down(step, half, owner):
        return remote(
            down_w.at[core, owner], down_w.at[half, owner],
            df_send.at[step - 1], df_recv.at[step - 1], sibling,
        )

    for step in range(1, n_dp):
        owner = lax.rem(dp + n_dp - step, n_dp)
        down_copy(step, owner).wait_recv()
        forward_down(step, core, owner).start()
    for step in range(1, n_dp):
        owner = lax.rem(dp + n_dp - step, n_dp)
        forward_down(step, 1 - core, owner).wait_recv()
        forward_down(step, core, owner).wait_send()
        down_copy(step, dp).wait_send()

    def far_place(origin):
        return (origin // RUN) * 2 + origin % 2

    def far_pieces(at, step, there, place):
        return (
            remote(
                out_rows.at[block(there), columns(at)], far_rows.at[block(place), columns(at)],
                b_send.at[at, step], f_recv.at[at, place], peer(step, 1 - sec),
            ),
            remote(
                out_ext.at[block(there), lanes(at)], far_ext.at[block(place), lanes(at)],
                b_send.at[at, EXPERTS + step], f_recv.at[at, far_blocks + place], peer(step, 1 - sec),
            ),
        )

    def send_back(at):
        def body(step, carry):
            there = lax.rem(chip + step, EXPERTS)
            far = is_far(there, chip)

            @pl.when(far == 0)
            def _():
                for copy in pieces(b_way, b_sems, at, step, there, chip):
                    copy.start()

            @pl.when(far == 1)
            def _():
                for copy in far_pieces(at, step, there, far_place(chip)):
                    copy.start()

            return carry

        lax.fori_loop(1, EXPERTS, body, 0)
        keep_own(b_way, at)

    def wait_near(at):
        def body(step, carry):
            origin = lax.rem(chip + EXPERTS - step, EXPERTS)

            @pl.when(is_far(chip, origin) == 0)
            def _():
                for copy in pieces(b_way, b_sems, at, step, origin, origin):
                    copy.wait_recv()

            return carry

        lax.fori_loop(1, EXPERTS, body, 0)

    def wait_far(at):
        def body(place, carry):
            for copy in far_pieces(at, 1, 0, place):
                copy.wait_recv()
            return carry

        lax.fori_loop(0, far_blocks, body, 0)

    @pl.when(sec == 0)
    def _():
        for at in range(QUARTERS):
            value = dot(rate[0], down_w[0, at]) + dot(rate[1], down_w[1, at])
            store_slots(at, value, out_rows, out_ext)
            send_back(at)

    meta_copy().wait()
    far_first, far_second, far_both, far_counts = routes(meta_recv[0:2, :], tokens)
    far_weights = far_first * meta_recv[2:3, :] + far_second * meta_recv[3:4, :]
    far_row = iota((far_slots, tokens), 0)
    far_head = far_row < far_heads
    far_block = jnp.where(far_head, far_row // HEAD, (far_row - far_heads) // TAIL)
    far_expert = (far_block // 2) * RUN + far_block % 2 + 2 * (1 - depth // 2)
    far_slot = jnp.where(far_head, far_row % HEAD, HEAD + far_row % TAIL)
    far_mix[...] = slots_of(far_expert, far_slot, far_both, far_counts, far_weights)[1].T.astype(BF16)

    for at in range(QUARTERS):
        wait_all(c_way, c_sems, at)
        unfold(at, c_rows, c_ext, unfold_all, rows, slots - rows)
        for half in range(2):
            part = dot_t(c_rows[:, columns(at)], down_w[half, at])
            rate_grad[half] = part if at == 0 else rate_grad[half] + part
    for half in range(2):
        gg[half] = (rate_grad[half] * der_gate[half]).astype(BF16)
        ug[half] = (rate_grad[half] * der_up[half]).astype(BF16)

    def dots_copy(step, there, landed_at):
        def tile(at):
            return pl.ds(pl.multiple_of(at * 8, 8), 8)

        return remote(
            dots.at[tile(there), :], dots_recv.at[tile(landed_at), :], v_send.at[step], v_recv.at[step], peer(step)
        )

    @pl.when(sec == 1)
    def _():
        for at in range(QUARTERS):
            value = dot_t(gg[0], gate_w[0, columns(at), :]) + dot_t(gg[1], gate_w[1, columns(at), :])
            value = value + dot_t(ug[0], up_w[0, columns(at), :]) + dot_t(ug[1], up_w[1, columns(at), :])
            store_slots(at, value * gain_ref[:, columns(at)], out_rows, out_ext)
            if at == 0:
                product = jnp.zeros((slots, 1), F32)
                for half in range(2):
                    terms = gg[half].astype(F32) * gate_act[half] + ug[half].astype(F32) * up_act[half]
                    product = product + jnp.sum(terms, axis=1, keepdims=True)
                placed = product * jnp.where(slot_at == iota((slots, tokens), 1), 1.0, 0.0)
                source_at = iota((8 * EXPERTS, slots), 1)
                source = jnp.where(source_at < rows, source_at // HEAD, (source_at - rows) // TAIL)
                group = jnp.where(source == iota((8 * EXPERTS, slots), 0) // 8, 1.0, 0.0)
                dots[...] = jnp.dot(
                    group, placed, precision=lax.Precision.HIGHEST, preferred_element_type=F32
                )

                def body(step, carry):
                    dots_copy(step, lax.rem(chip + step, EXPERTS), chip).start()
                    return carry

                lax.fori_loop(1, EXPERTS, body, 0)
                tile = pl.ds(pl.multiple_of(chip * 8, 8), 8)
                dots_recv[tile, :] = dots[tile, :]
            send_back(at)

    def sib_copy(step, at):
        part = pl.ds(pl.multiple_of(at * shard, shard), shard)
        return remote(sib_term.at[part, :], sib_recv.at[part, :], t_send.at[step], t_recv.at[step], sibling)

    def rep_copy(step, at):
        part = pl.ds(pl.multiple_of(at * shard, shard), shard)
        return remote(
            sib_recv.at[part, :], rep_recv.at[step - 1], r_send.at[step - 1], r_recv.at[step - 1], replica(step)
        )

    halves = shard // 2
    for step in range(n_dp + 1):
        if step < n_dp:
            at = lax.rem(dp + step + 1, n_dp)
            for piece in range(2):
                low = piece * halves
                part = pl.ds(pl.multiple_of(at * shard + low, halves), halves)
                own_term[step % 2, low : low + halves, :] = t_dot(x_rows[:, part], ug[core])
                sib_term[part, :] = t_dot(x_rows[:, part], ug[1 - core]).astype(BF16)
            sib_copy(step, at).start()
        if step > 0:
            at = lax.rem(dp + step, n_dp)
            sib_copy(step - 1, at).wait()
            part = pl.ds(pl.multiple_of(at * shard, shard), shard)
            sib_recv[part, :] = (own_term[(step - 1) % 2] + sib_recv[part, :].astype(F32)).astype(BF16)
            if step < n_dp:
                rep_copy(step, at).start()

    def pass_copy(at):
        return remote(
            final.at[:, columns(at)], landed.at[:, columns(at)], s_send.at[at], s_recv.at[at], across
        )

    def pass_on(at, base):
        wait_near(at)
        unfold(at, back_rows, back_ext, unfold_all, rows, slots - rows)
        final[:, columns(at)] = (base + dot(mix[...], back_rows[:, columns(at)])).astype(BF16)
        pass_copy(at).start()

    @pl.when(sec == 0)
    def _():
        for at in range(QUARTERS):
            pass_on(at, act_ref[:, columns(at)].astype(F32))

    @pl.when(sec == 1)
    def _():
        def body(step, carry):
            origin = lax.rem(chip + EXPERTS - step, EXPERTS)
            dots_copy(step, origin, origin).wait_recv()
            return carry

        lax.fori_loop(1, EXPERTS, body, 0)
        spread = jnp.where(
            expert_at[:, 0:1] * 8 == iota((slots, 8 * EXPERTS), 1), 1.0, 0.0
        )
        by_slot = jnp.dot(
            spread, dots_recv[...], precision=lax.Precision.HIGHEST, preferred_element_type=F32
        )
        product = jnp.sum(
            jnp.where(slot_at == iota((slots, tokens), 1), by_slot, 0.0), axis=1, keepdims=True
        )
        token_row = jnp.sum(taken * product, axis=0, keepdims=True)
        token_dot = jnp.sum(one * token_row, axis=1, keepdims=True)
        scale = inv_rms * inv_rms * token_dot / width
        for at in range(QUARTERS):
            cols = columns(at)
            pass_on(at, cot_ref[:, cols].astype(F32) - act_ref[:, cols].astype(F32) * scale)

    for step in range(1, n_dp):
        rep_copy(step, dp).wait_recv()
    own = pl.ds(pl.multiple_of(dp * shard, shard), shard)
    total_grad = sib_recv[own, :].astype(F32)
    for step in range(1, n_dp):
        total_grad = total_grad + rep_recv[step - 1].astype(F32)
    upgrad_ref[...] = total_grad.astype(BF16)

    edge = at_edge(depth)

    @pl.when(edge == 0)
    def _():
        for at in range(QUARTERS):
            pass_copy(at).wait()
            res_ref[:, columns(at)] = landed[:, columns(at)]

    @pl.when(edge == 1)
    def _():
        unfold_far = fold_order(far_blocks, False)
        for at in range(QUARTERS):
            wait_far(at)
            unfold(at, far_rows, far_ext, unfold_far, far_heads, far_slots - far_heads)
            direct = dot(far_mix[...], far_rows[:, columns(at)])
            pass_copy(at).wait()
            res_ref[:, columns(at)] = (landed[:, columns(at)].astype(F32) + direct).astype(BF16)

    wait_sent(x_way, x_sems)
    wait_sent(c_way, c_sems)
    wait_sent(b_way, b_sems)

    @pl.when(sec == 1)
    def _():
        def body(step, carry):
            dots_copy(step, lax.rem(chip + step, EXPERTS), chip).wait_send()
            return carry

        lax.fori_loop(1, EXPERTS, body, 0)

    for step in range(1, n_dp):
        rep_copy(step, dp).wait_send()


def per_device(
    activations, norm_gain, route_ids, route_gates, gate_weight, up_weight, leak_rates, down_weight, cotangent
):
    tokens, width = activations.shape[1:]
    hidden = gate_weight.shape[2]
    shard = down_weight.shape[2]
    n_dp = lax.axis_size("dp")
    rows = EXPERTS * HEAD
    slots = rows + EXPERTS * TAIL
    fold = width // FOLDS
    vmem = pl.BlockSpec(memory_space=pltpu.VMEM)
    anywhere = pl.BlockSpec(memory_space=pl.ANY)
    dma = pltpu.SemaphoreType.DMA

    def scratch(kind, *shape):
        return pltpu.VMEM(shape, kind)

    result, up_grad = pl.pallas_call(
        kernel,
        out_shape=(
            jax.ShapeDtypeStruct((tokens, width), BF16),
            jax.ShapeDtypeStruct((shard, hidden), BF16),
        ),
        in_specs=[vmem] * 6 + [anywhere] * 3,
        out_specs=(vmem, vmem),
        scratch_shapes=[
            scratch(BF16, 2, width, hidden),
            scratch(BF16, 2, width, hidden),
            scratch(BF16, 2, n_dp, hidden, shard),
            scratch(F32, 2, 8, hidden),
            scratch(BF16, rows, width),
            scratch(BF16, rows, fold),
            scratch(BF16, rows, width),
            scratch(BF16, rows, fold),
            scratch(BF16, slots, width),
            scratch(BF16, rows, fold),
            scratch(BF16, slots, width),
            scratch(BF16, rows, fold),
            scratch(F32, 2, slots, hidden),
            scratch(F32, 2, slots, hidden),
            scratch(BF16, 2, slots, hidden),
            scratch(F32, 2, slots, hidden),
            scratch(F32, 2, slots, hidden),
            scratch(F32, 2, slots, hidden),
            scratch(BF16, rows, width),
            scratch(BF16, rows, fold),
            scratch(BF16, slots, width),
            scratch(BF16, rows, fold),
            scratch(BF16, slots // 2, width),
            scratch(BF16, rows // 2, fold),
            scratch(BF16, tokens, width),
            scratch(BF16, tokens, width),
            scratch(F32, 8, tokens),
            scratch(F32, 8, tokens),
            scratch(F32, 8 * EXPERTS, tokens),
            scratch(F32, 8 * EXPERTS, tokens),
            scratch(BF16, tokens, slots),
            scratch(BF16, tokens, slots // 2),
            scratch(F32, 2, shard, hidden),
            scratch(BF16, width, hidden),
            scratch(BF16, width, hidden),
            scratch(BF16, n_dp - 1, shard, hidden),
            scratch(BF16, 2, slots, hidden),
            scratch(BF16, 2, slots, hidden),
            dma((4,)), dma((4,)), dma((4,)),
            dma((n_dp - 1,)), dma((n_dp - 1,)), dma((n_dp - 1,)), dma((n_dp - 1,)),
            *([dma((QUARTERS, 2 * EXPERTS))] * 6), dma((QUARTERS, EXPERTS)),
            dma((QUARTERS,)), dma((QUARTERS,)), dma((n_dp,)), dma((n_dp,)),
            dma((n_dp - 1,)), dma((n_dp - 1,)), dma((1,)), dma((1,)), dma((EXPERTS,)), dma((EXPERTS,)),
        ],
        compiler_params=pltpu.CompilerParams(
            collective_id=0, has_side_effects=True, vmem_limit_bytes=60 * 2**20
        ),
    )(
        activations[0],
        cotangent[0],
        norm_gain,
        route_ids[0].T,
        route_gates[0].T,
        jnp.broadcast_to(leak_rates, (8, hidden)),
        gate_weight[0],
        up_weight[0],
        down_weight[0],
    )
    first = lax.axis_index("section") == 0
    nothing = jnp.zeros_like(result)
    passed_on = jnp.where(first, nothing, result)
    passed_back = jnp.where(first, result, nothing)
    return (passed_on[None], passed_back[None], up_grad[None])


def solution(mesh):
    return jax.shard_map(
        per_device,
        mesh=mesh,
        in_specs=(
            P("section", ("dp", "expert"), None),
            P("section", None),
            P("section", ("dp", "expert"), None),
            P("section", ("dp", "expert"), None),
            P("section", None, "expert"),
            P("section", None, "expert"),
            P("section", "expert"),
            P("section", "expert", "dp"),
            P("section", ("dp", "expert"), None),
        ),
        out_specs=(
            P("section", ("dp", "expert"), None),
            P("section", ("dp", "expert"), None),
            P("section", "dp", "expert"),
        ),
        check_vma=False,
    )
```

time: 260 us -> 212 us (0.82)
  the two profiles are of different devices: /device:TPU:104 before, /device:TPU:66 now
where the time goes in v2:
time: 212 us
  Pallas kernels  206 us (97%)
  other arithmetic  3.46 us (2%)
    pallas_call x1, Pallas kernels, per_device(): pl.pallas_call(kernel, out_shape=(jax.ShapeDtypeStruct((tokens, width), B...  206 us

profile of v2, /device:TPU:66, one launch (start us, length us, event | category | flops | bytes accessed | tf_op | source)
XLA Modules:
  0.0 211.9 jit_solution(655766910449169877)
XLA Ops:
  0.6 0.7 reduce
  1.3 0.6 broadcast_in_dim.21.leak_ref
  1.9 206.3 %shard_map.112 = (bf16[128,4096]{1,0:T(8,128)(2,1)}, bf16[1024,384]{1,0:T(8,128)(2,1)}) custom-call(bf16[128,4096]{1,0:T(8,128)(2,1)} %bitcast.18, bf16[128,4096]{1,0:T(8,128)(2,1)} %bitcast.19, f32[1,4096]{1,0:T(1,128)} %gain_ref.1, s32[2,128]{1,0:T(2,128)} %bitcast.22, f32[2,128]{1,0:T(2,128)} %bitcast.23, f32[8,384]{1,0:T(8,128)} %broadcast_in_dim.21.leak_ref, ...), custom_call_target="tpu_custom_call" | custom-call | tf_op jit(solution)/shard_map/pallas_call | solution.py:613
  208.2 0.0 copy-start
  208.2 2.8 %select_bitcast_fusion = (bf16[1,128,4096]{2,1,0:T(8,128)(2,1)}, bf16[1,128,4096]{2,1,0:T(8,128)(2,1)}) fusion(bf16[128,4096]{1,0:T(8,128)(2,1)} %get-tuple-element.5, pred[]{:T(512)S(6)} %eq.3), kind=kLoop, calls=%fused_computation | loop fusion | flops 1048576 | bytes 3145729 | tf_op jit(solution)/shard_map/broadcast_in_dim | solution.py:684
  211.0 0.0 copy-done
  211.0 0.9 copy.13
Async XLA Ops:
  208.2 2.8 %copy-start = (bf16[1024,384]{1,0:T(8,128)(2,1)S(1)}, bf16[1024,384]{1,0:T(8,128)(2,1)}, u32[]{:S(2)}) copy-start(bf16[1024,384]{1,0:T(8,128)(2,1)} %get-tuple-element.6) | copy-start | bytes 2359300

commit v3 on v2

--- a/solution.py
+++ b/solution.py
@@ -78,10 +78,9 @@
     act_ref, cot_ref, gain_ref, ids_ref, gates_ref, leak_ref, gate_hbm, up_hbm, down_hbm,
     res_ref, upgrad_ref,
     gate_w, up_w, down_w, leak_w,
-    send_x, send_xe, send_c, send_ce,
-    x_rows, x_ext, c_rows, c_ext,
+    send_x, send_c, x_rows, c_rows,
     gate_act, up_act, rate, der_gate, der_up, rate_grad,
-    out_rows, out_ext, back_rows, back_ext, far_rows, far_ext,
+    out_rows, back_rows, far_rows,
     final, landed, meta, meta_recv, dots, dots_recv, mix, far_mix,
     own_term, sib_term, sib_recv, rep_recv,
     gg, ug,
@@ -132,10 +131,19 @@
 
     def greet(step, carry):
         pl.semaphore_signal(barrier, inc=1, device_id=peer(step), device_id_type=MESH)
-        pl.semaphore_signal(barrier, inc=1, device_id=peer(step, 1 - sec), device_id_type=MESH)
         return carry
 
+    def greet_far(step, carry):
+        there = lax.rem(chip + step, EXPERTS)
+
+        @pl.when(is_far(there, chip) + is_far(chip, there) > 0)
+        def _():
+            pl.semaphore_signal(barrier, inc=1, device_id=peer(step, 1 - sec), device_id_type=MESH)
+
+        return carry
+
     lax.fori_loop(1, EXPERTS, greet, 0)
+    lax.fori_loop(1, EXPERTS, greet_far, 0)
     for step in range(1, n_dp):
         pl.semaphore_signal(barrier, inc=1, device_id=replica(step), device_id_type=MESH)
     pl.semaphore_signal(barrier, inc=1, device_id=sibling, device_id_type=MESH)
@@ -161,71 +169,65 @@
     def columns(at):
         return slice(at * quarter, (at + 1) * quarter)
 
-    def lanes(at):
-        return slice(at * LANES, (at + 1) * LANES)
+    pitch = quarter + LANES
+
+    def heads(at):
+        return slice(at * pitch, at * pitch + quarter)
+
+    def tails(at):
+        return slice(at * pitch + quarter, (at + 1) * pitch)
+
+    def span(at):
+        return slice(at * pitch, (at + 1) * pitch)
 
     def block(at):
         return pl.ds(pl.multiple_of(at * HEAD, HEAD), HEAD)
 
-    def store_slots(at, value, head_ref, ext_ref):
-        head_ref[0:rows, columns(at)] = value[0:rows].astype(BF16)
-        ext_ref[:, lanes(at)] = dot(fold_up, folds(value[rows:slots].astype(BF16))).astype(BF16)
-
-    def unfold(at, head_ref, ext_ref, order, heads, tails):
-        back = dot(order, ext_ref[:, lanes(at)]).astype(BF16)
+    def store_slots(at, value, ref):
+        ref[0:rows, heads(at)] = value[0:rows].astype(BF16)
+        ref[0:rows, tails(at)] = dot(fold_up, folds(value[rows:slots].astype(BF16))).astype(BF16)
+
+    def unfold(at, ref, order, first_row, count):
+        back = dot(order, ref[0:first_row, tails(at)]).astype(BF16)
         for fold in range(FOLDS):
-            low = at * quarter + fold * LANES
-            head_ref[heads : heads + tails, low : low + LANES] = back[fold * tails : (fold + 1) * tails]
-
-    def pieces(way, sems, at, step, there, landed_at):
-        src, dst, ext_src, ext_dst = way
+            low = at * pitch + fold * LANES
+            ref[first_row : first_row + count, low : low + LANES] = back[fold * count : (fold + 1) * count]
+
+    def piece(way, sems, at, step, there, landed_at):
+        src, dst = way
         send, recv = sems
-        return (
-            remote(
-                src.at[block(there), columns(at)], dst.at[block(landed_at), columns(at)],
-                send.at[at, step], recv.at[at, step], peer(step),
-            ),
-            remote(
-                ext_src.at[block(there), lanes(at)], ext_dst.at[block(landed_at), lanes(at)],
-                send.at[at, EXPERTS + step], recv.at[at, EXPERTS + step], peer(step),
-            ),
+        return remote(
+            src.at[block(there), span(at)], dst.at[block(landed_at), span(at)], send.at[at], recv.at[at], peer(step)
+        )
+
+    def bulk(way, sems, at, blocks):
+        src, dst = way
+        send, recv = sems
+        return remote(
+            src.at[0 : blocks * HEAD, span(at)], dst.at[0 : blocks * HEAD, span(at)], send.at[at], recv.at[at], peer(1)
         )
 
     def send_all(way, sems, at):
         def body(step, carry):
-            for copy in pieces(way, sems, at, step, lax.rem(chip + step, EXPERTS), chip):
-                copy.start()
+            piece(way, sems, at, step, lax.rem(chip + step, EXPERTS), chip).start()
             return carry
 
         lax.fori_loop(1, EXPERTS, body, 0)
 
     def wait_all(way, sems, at):
-        def body(step, carry):
-            origin = lax.rem(chip + EXPERTS - step, EXPERTS)
-            for copy in pieces(way, sems, at, step, origin, origin):
-                copy.wait_recv()
-            return carry
-
-        lax.fori_loop(1, EXPERTS, body, 0)
+        bulk(way, sems, at, EXPERTS - 1).wait_recv()
 
     def wait_sent(way, sems):
         for at in range(QUARTERS):
-
-            def body(step, carry):
-                for copy in pieces(way, sems, at, step, lax.rem(chip + step, EXPERTS), chip):
-                    copy.wait_send()
-                return carry
-
-            lax.fori_loop(1, EXPERTS, body, 0)
+            bulk(way, sems, at, EXPERTS - 1).wait_send()
 
     def keep_own(way, at):
-        src, dst, ext_src, ext_dst = way
-        dst[block(chip), columns(at)] = src[block(chip), columns(at)]
-        ext_dst[block(chip), lanes(at)] = ext_src[block(chip), lanes(at)]
-
-    x_way, x_sems = (send_x, x_rows, send_xe, x_ext), (x_send, x_recv)
-    c_way, c_sems = (send_c, c_rows, send_ce, c_ext), (c_send, c_recv)
-    b_way, b_sems = (out_rows, back_rows, out_ext, back_ext), (b_send, b_recv)
+        src, dst = way
+        dst[block(chip), span(at)] = src[block(chip), span(at)]
+
+    x_way, x_sems = (send_x, x_rows), (x_send, x_recv)
+    c_way, c_sems = (send_c, c_rows), (c_send, c_recv)
+    b_way, b_sems = (out_rows, back_rows), (b_send, b_recv)
 
     own_weights = [
         pltpu.make_async_copy(gate_hbm, gate_w.at[core], w_own_sem.at[0]),
@@ -253,10 +255,10 @@
     def prepare(at):
         cols = columns(at)
         normed = (act_ref[:, cols].astype(F32) * inv_rms * gain_ref[:, cols]).astype(BF16)
-        store_slots(at, dot(pick, normed), send_x, send_xe)
+        store_slots(at, dot(pick, normed), send_x)
 
     prepare(0)
-    pl.semaphore_wait(barrier, 2 * (EXPERTS - 1) + n_dp - 1 + 2)
+    pl.semaphore_wait(barrier, EXPERTS - 1 + n_dp - 1 + 2 + RUN + RUN * at_edge(depth))
     send_all(x_way, x_sems, 0)
 
     for copy in own_weights:
@@ -269,12 +271,16 @@
     for at in range(1, QUARTERS):
         prepare(at)
         send_all(x_way, x_sems, at)
-    for at in range(QUARTERS):
-        store_slots(at, dot(pick, cot_ref[:, columns(at)]) * slot_gate, send_c, send_ce)
+
+    def send_grads(at):
+        store_slots(at, dot(pick, cot_ref[:, columns(at)]) * slot_gate, send_c)
         send_all(c_way, c_sems, at)
+        keep_own(c_way, at)
+
+    for at in range(QUARTERS // 2):
+        send_grads(at)
     for at in range(QUARTERS):
         keep_own(x_way, at)
-        keep_own(c_way, at)
 
     one = jnp.where(iota((tokens, tokens), 0) == iota((tokens, tokens), 1), 1.0, 0.0)
     inv_row = jnp.sum(one * inv_rms, axis=0, keepdims=True)
@@ -291,8 +297,7 @@
     def clear(origin, carry):
         @pl.when(is_far(chip, origin) == 1)
         def _():
-            back_rows[block(origin), :] = jnp.zeros((HEAD, width), BF16)
-            back_ext[block(origin), :] = jnp.zeros((HEAD, QUARTERS * LANES), BF16)
+            back_rows[block(origin), :] = jnp.zeros((HEAD, QUARTERS * pitch), BF16)
 
         return carry
 
@@ -307,10 +312,10 @@
 
     for at in range(QUARTERS):
         wait_all(x_way, x_sems, at)
-        unfold(at, x_rows, x_ext, unfold_all, rows, slots - rows)
+        unfold(at, x_rows, unfold_all, rows, slots - rows)
         for half in range(2):
             for weight, total in ((gate_w, gate_act), (up_w, up_act)):
-                part = dot(x_rows[:, columns(at)], weight[half, columns(at), :])
+                part = dot(x_rows[:, heads(at)], weight[half, columns(at), :])
                 total[half] = part if at == 0 else total[half] + part
 
     for half in range(2):
@@ -367,18 +372,6 @@
     def far_place(origin):
         return (origin // RUN) * 2 + origin % 2
 
-    def far_pieces(at, step, there, place):
-        return (
-            remote(
-                out_rows.at[block(there), columns(at)], far_rows.at[block(place), columns(at)],
-                b_send.at[at, step], f_recv.at[at, place], peer(step, 1 - sec),
-            ),
-            remote(
-                out_ext.at[block(there), lanes(at)], far_ext.at[block(place), lanes(at)],
-                b_send.at[at, EXPERTS + step], f_recv.at[at, far_blocks + place], peer(step, 1 - sec),
-            ),
-        )
-
     def send_back(at):
         def body(step, carry):
             there = lax.rem(chip + step, EXPERTS)
@@ -386,13 +379,14 @@
 
             @pl.when(far == 0)
             def _():
-                for copy in pieces(b_way, b_sems, at, step, there, chip):
-                    copy.start()
+                piece(b_way, b_sems, at, step, there, chip).start()
 
             @pl.when(far == 1)
             def _():
-                for copy in far_pieces(at, step, there, far_place(chip)):
-                    copy.start()
+                remote(
+                    out_rows.at[block(there), span(at)], far_rows.at[block(far_place(chip)), span(at)],
+                    b_send.at[at], f_recv.at[at], peer(step, 1 - sec),
+                ).start()
 
             return carry
 
@@ -400,32 +394,26 @@
         keep_own(b_way, at)
 
     def wait_near(at):
-        def body(step, carry):
-            origin = lax.rem(chip + EXPERTS - step, EXPERTS)
-
-            @pl.when(is_far(chip, origin) == 0)
-            def _():
-                for copy in pieces(b_way, b_sems, at, step, origin, origin):
-                    copy.wait_recv()
-
-            return carry
-
-        lax.fori_loop(1, EXPERTS, body, 0)
+        @pl.when(at_edge(depth) == 0)
+        def _():
+            bulk(b_way, b_sems, at, EXPERTS - 1).wait_recv()
+
+        @pl.when(at_edge(depth) == 1)
+        def _():
+            bulk(b_way, b_sems, at, EXPERTS - 1 - far_blocks).wait_recv()
 
     def wait_far(at):
-        def body(place, carry):
-            for copy in far_pieces(at, 1, 0, place):
-                copy.wait_recv()
-            return carry
-
-        lax.fori_loop(0, far_blocks, body, 0)
+        bulk((out_rows, far_rows), (b_send, f_recv), at, far_blocks).wait_recv()
 
     @pl.when(sec == 0)
     def _():
         for at in range(QUARTERS):
             value = dot(rate[0], down_w[0, at]) + dot(rate[1], down_w[1, at])
-            store_slots(at, value, out_rows, out_ext)
+            store_slots(at, value, out_rows)
             send_back(at)
+
+    for at in range(QUARTERS // 2, QUARTERS):
+        send_grads(at)
 
     meta_copy().wait()
     far_first, far_second, far_both, far_counts = routes(meta_recv[0:2, :], tokens)
@@ -439,9 +427,9 @@
 
     for at in range(QUARTERS):
         wait_all(c_way, c_sems, at)
-        unfold(at, c_rows, c_ext, unfold_all, rows, slots - rows)
+        unfold(at, c_rows, unfold_all, rows, slots - rows)
         for half in range(2):
-            part = dot_t(c_rows[:, columns(at)], down_w[half, at])
+            part = dot_t(c_rows[:, heads(at)], down_w[half, at])
             rate_grad[half] = part if at == 0 else rate_grad[half] + part
     for half in range(2):
         gg[half] = (rate_grad[half] * der_gate[half]).astype(BF16)
@@ -452,15 +440,19 @@
             return pl.ds(pl.multiple_of(at * 8, 8), 8)
 
         return remote(
-            dots.at[tile(there), :], dots_recv.at[tile(landed_at), :], v_send.at[step], v_recv.at[step], peer(step)
-        )
+            dots.at[tile(there), :], dots_recv.at[tile(landed_at), :], v_send.at[0], v_recv.at[0], peer(step)
+        )
+
+    def dots_bulk():
+        part = slice(0, 8 * (EXPERTS - 1))
+        return remote(dots.at[part, :], dots_recv.at[part, :], v_send.at[0], v_recv.at[0], peer(1))
 
     @pl.when(sec == 1)
     def _():
         for at in range(QUARTERS):
             value = dot_t(gg[0], gate_w[0, columns(at), :]) + dot_t(gg[1], gate_w[1, columns(at), :])
             value = value + dot_t(ug[0], up_w[0, columns(at), :]) + dot_t(ug[1], up_w[1, columns(at), :])
-            store_slots(at, value * gain_ref[:, columns(at)], out_rows, out_ext)
+            store_slots(at, value * gain_ref[:, columns(at)], out_rows)
             if at == 0:
                 product = jnp.zeros((slots, 1), F32)
                 for half in range(2):
@@ -500,8 +492,9 @@
             for piece in range(2):
                 low = piece * halves
                 part = pl.ds(pl.multiple_of(at * shard + low, halves), halves)
-                own_term[step % 2, low : low + halves, :] = t_dot(x_rows[:, part], ug[core])
-                sib_term[part, :] = t_dot(x_rows[:, part], ug[1 - core]).astype(BF16)
+                normed = x_rows[:, pl.ds(pl.multiple_of(at * pitch + low, LANES), halves)]
+                own_term[step % 2, low : low + halves, :] = t_dot(normed, ug[core])
+                sib_term[part, :] = t_dot(normed, ug[1 - core]).astype(BF16)
             sib_copy(step, at).start()
         if step > 0:
             at = lax.rem(dp + step, n_dp)
@@ -518,8 +511,8 @@
 
     def pass_on(at, base):
         wait_near(at)
-        unfold(at, back_rows, back_ext, unfold_all, rows, slots - rows)
-        final[:, columns(at)] = (base + dot(mix[...], back_rows[:, columns(at)])).astype(BF16)
+        unfold(at, back_rows, unfold_all, rows, slots - rows)
+        final[:, columns(at)] = (base + dot(mix[...], back_rows[:, heads(at)])).astype(BF16)
         pass_copy(at).start()
 
     @pl.when(sec == 0)
@@ -529,12 +522,7 @@
 
     @pl.when(sec == 1)
     def _():
-        def body(step, carry):
-            origin = lax.rem(chip + EXPERTS - step, EXPERTS)
-            dots_copy(step, origin, origin).wait_recv()
-            return carry
-
-        lax.fori_loop(1, EXPERTS, body, 0)
+        dots_bulk().wait_recv()
         spread = jnp.where(
             expert_at[:, 0:1] * 8 == iota((slots, 8 * EXPERTS), 1), 1.0, 0.0
         )
@@ -572,8 +560,8 @@
         unfold_far = fold_order(far_blocks, False)
         for at in range(QUARTERS):
             wait_far(at)
-            unfold(at, far_rows, far_ext, unfold_far, far_heads, far_slots - far_heads)
-            direct = dot(far_mix[...], far_rows[:, columns(at)])
+            unfold(at, far_rows, unfold_far, far_heads, far_slots - far_heads)
+            direct = dot(far_mix[...], far_rows[:, heads(at)])
             pass_copy(at).wait()
             res_ref[:, columns(at)] = (landed[:, columns(at)].astype(F32) + direct).astype(BF16)
 
@@ -583,11 +571,7 @@
 
     @pl.when(sec == 1)
     def _():
-        def body(step, carry):
-            dots_copy(step, lax.rem(chip + step, EXPERTS), chip).wait_send()
-            return carry
-
-        lax.fori_loop(1, EXPERTS, body, 0)
+        dots_bulk().wait_send()
 
     for step in range(1, n_dp):
         rep_copy(step, dp).wait_send()
@@ -602,7 +586,7 @@
     n_dp = lax.axis_size("dp")
     rows = EXPERTS * HEAD
     slots = rows + EXPERTS * TAIL
-    fold = width // FOLDS
+    pitched = width + QUARTERS * LANES
     vmem = pl.BlockSpec(memory_space=pltpu.VMEM)
     anywhere = pl.BlockSpec(memory_space=pl.ANY)
     dma = pltpu.SemaphoreType.DMA
@@ -623,26 +607,19 @@
             scratch(BF16, 2, width, hidden),
             scratch(BF16, 2, n_dp, hidden, shard),
             scratch(F32, 2, 8, hidden),
-            scratch(BF16, rows, width),
-            scratch(BF16, rows, fold),
-            scratch(BF16, rows, width),
-            scratch(BF16, rows, fold),
-            scratch(BF16, slots, width),
-            scratch(BF16, rows, fold),
-            scratch(BF16, slots, width),
-            scratch(BF16, rows, fold),
+            scratch(BF16, rows, pitched),
+            scratch(BF16, rows, pitched),
+            scratch(BF16, slots, pitched),
+            scratch(BF16, slots, pitched),
             scratch(F32, 2, slots, hidden),
             scratch(F32, 2, slots, hidden),
             scratch(BF16, 2, slots, hidden),
             scratch(F32, 2, slots, hidden),
             scratch(F32, 2, slots, hidden),
             scratch(F32, 2, slots, hidden),
-            scratch(BF16, rows, width),
-            scratch(BF16, rows, fold),
-            scratch(BF16, slots, width),
-            scratch(BF16, rows, fold),
-            scratch(BF16, slots // 2, width),
-            scratch(BF16, rows // 2, fold),
+            scratch(BF16, rows, pitched),
+            scratch(BF16, slots, pitched),
+            scratch(BF16, slots // 2, pitched),
             scratch(BF16, tokens, width),
             scratch(BF16, tokens, width),
             scratch(F32, 8, tokens),
@@ -659,9 +636,9 @@
             scratch(BF16, 2, slots, hidden),
             dma((4,)), dma((4,)), dma((4,)),
             dma((n_dp - 1,)), dma((n_dp - 1,)), dma((n_dp - 1,)), dma((n_dp - 1,)),
-            *([dma((QUARTERS, 2 * EXPERTS))] * 6), dma((QUARTERS, EXPERTS)),
+            *([dma((QUARTERS,))] * 7),
             dma((QUARTERS,)), dma((QUARTERS,)), dma((n_dp,)), dma((n_dp,)),
-            dma((n_dp - 1,)), dma((n_dp - 1,)), dma((1,)), dma((1,)), dma((EXPERTS,)), dma((EXPERTS,)),
+            dma((n_dp - 1,)), dma((n_dp - 1,)), dma((1,)), dma((1,)), dma((1,)), dma((1,)),
         ],
         compiler_params=pltpu.CompilerParams(
             collective_id=0, has_side_effects=True, vmem_limit_bytes=60 * 2**20

time: 212 us -> 204 us (0.962)
  the two profiles are of different devices: /device:TPU:66 before, /device:TPU:32 now
where the time goes in v3:
time: 204 us; the launch traced here: 203 us
  Pallas kernels  198 us (97%)
  other arithmetic  3.46 us (2%)
    pallas_call x1, Pallas kernels, per_device(): pl.pallas_call(kernel, out_shape=(jax.ShapeDtypeStruct((tokens, width), B...  198 us

profile of v3, /device:TPU:32, one launch (start us, length us, event | category | flops | bytes accessed | tf_op | source)
XLA Modules:
  0.0 203.3 jit_solution(17667328587318282082)
XLA Ops:
  0.6 0.7 reduce
  1.3 0.6 broadcast_in_dim.21.leak_ref
  1.9 197.7 %shard_map.112 = (bf16[128,4096]{1,0:T(8,128)(2,1)}, bf16[1024,384]{1,0:T(8,128)(2,1)}) custom-call(bf16[128,4096]{1,0:T(8,128)(2,1)} %bitcast.18, bf16[128,4096]{1,0:T(8,128)(2,1)} %bitcast.19, f32[1,4096]{1,0:T(1,128)} %gain_ref.1, s32[2,128]{1,0:T(2,128)} %bitcast.22, f32[2,128]{1,0:T(2,128)} %bitcast.23, f32[8,384]{1,0:T(8,128)} %broadcast_in_dim.21.leak_ref, ...), custom_call_target="tpu_custom_call" | custom-call | tf_op jit(solution)/shard_map/pallas_call | solution.py:597
  199.6 0.0 copy-start
  199.7 2.8 %select_bitcast_fusion = (bf16[1,128,4096]{2,1,0:T(8,128)(2,1)}, bf16[1,128,4096]{2,1,0:T(8,128)(2,1)}) fusion(bf16[128,4096]{1,0:T(8,128)(2,1)} %get-tuple-element.5, pred[]{:T(512)S(6)} %eq.3), kind=kLoop, calls=%fused_computation | loop fusion | flops 1048576 | bytes 3145729 | tf_op jit(solution)/shard_map/broadcast_in_dim | solution.py:661
  202.4 0.0 copy-done
  202.4 0.9 copy.13
Async XLA Ops:
  199.6 2.8 %copy-start = (bf16[1024,384]{1,0:T(8,128)(2,1)S(1)}, bf16[1024,384]{1,0:T(8,128)(2,1)}, u32[]{:S(2)}) copy-start(bf16[1024,384]{1,0:T(8,128)(2,1)} %get-tuple-element.6) | copy-start | bytes 2359300

commit v4 on v3

--- a/solution.py
+++ b/solution.py
@@ -17,6 +17,7 @@
 FOLDS = 8
 LANES = 128
 QUARTERS = 4
+GROUPS = 2
 EXPERTS = 16
 RUN = 4
 F32 = jnp.float32
@@ -75,8 +76,9 @@
 
 
 def kernel(
-    act_ref, cot_ref, gain_ref, ids_ref, gates_ref, leak_ref, gate_hbm, up_hbm, down_hbm,
-    res_ref, upgrad_ref,
+    gain_ref, ids_ref, gates_ref, act_hbm, cot_hbm, leak_hbm, gate_hbm, up_hbm, down_hbm,
+    passed_on_hbm, passed_back_hbm, up_grad_hbm,
+    act_ref, cot_ref, nothing,
     gate_w, up_w, down_w, leak_w,
     send_x, send_c, x_rows, c_rows,
     gate_act, up_act, rate, der_gate, der_up, rate_grad,
@@ -87,6 +89,7 @@
     w_own_sem, w_sib_send, w_sib_recv, d_send, d_recv, df_send, df_recv,
     x_send, x_recv, c_send, c_recv, b_send, b_recv, f_recv,
     s_send, s_recv, t_send, t_recv, r_send, r_recv, m_send, m_recv, v_send, v_recv,
+    in_sem, out_sem,
 ):
     sec = lax.axis_index("section")
     dp = lax.axis_index("dp")
@@ -127,6 +130,9 @@
             device_id=target, device_id_type=MESH,
         )
 
+    act_in = pltpu.make_async_copy(act_hbm, act_ref, in_sem.at[0])
+    cot_in = pltpu.make_async_copy(cot_hbm, cot_ref, in_sem.at[1])
+    act_in.start()
     barrier = pltpu.get_barrier_semaphore()
 
     def greet(step, carry):
@@ -162,7 +168,14 @@
     pick = taken.astype(BF16)
     fold_up = fold_order(EXPERTS, True)
     unfold_all = fold_order(EXPERTS, False)
-
+    per_group = EXPERTS // GROUPS
+    group_heads = per_group * HEAD
+    group_rows = slots // GROUPS
+    fold_group = fold_order(per_group, True)
+    unfold_group = fold_order(per_group, False)
+
+    act_in.wait()
+    cot_in.start()
     acts = act_ref[...].astype(F32)
     inv_rms = lax.rsqrt(jnp.mean(acts * acts, axis=-1, keepdims=True) + EPS)
 
@@ -182,58 +195,90 @@
 
     def block(at):
         return pl.ds(pl.multiple_of(at * HEAD, HEAD), HEAD)
+
+    def spot(step):
+        return pl.ds(pl.multiple_of((step // per_group) * group_rows + (step % per_group) * HEAD, HEAD), HEAD)
+
+    def group(at):
+        return slice(at * group_rows, (at + 1) * group_rows)
+
+    def store_group(which, at, value, ref):
+        part = slice(which * group_heads, (which + 1) * group_heads)
+        ref[part, heads(at)] = value[0:group_heads].astype(BF16)
+        ref[part, tails(at)] = dot(fold_group, folds(value[group_heads:group_rows].astype(BF16))).astype(BF16)
 
     def store_slots(at, value, ref):
         ref[0:rows, heads(at)] = value[0:rows].astype(BF16)
         ref[0:rows, tails(at)] = dot(fold_up, folds(value[rows:slots].astype(BF16))).astype(BF16)
 
-    def unfold(at, ref, order, first_row, count):
-        back = dot(order, ref[0:first_row, tails(at)]).astype(BF16)
+    def unfold(at, ref, order, first_row, count, base=0):
+        back = dot(order, ref[base : base + first_row, tails(at)]).astype(BF16)
+        start = base + first_row
         for fold in range(FOLDS):
             low = at * pitch + fold * LANES
-            ref[first_row : first_row + count, low : low + LANES] = back[fold * count : (fold + 1) * count]
-
-    def piece(way, sems, at, step, there, landed_at):
+            ref[start : start + count, low : low + LANES] = back[fold * count : (fold + 1) * count]
+
+    def unfold_slots(which, at, ref):
+        unfold(at, ref, unfold_group, group_heads, group_rows - group_heads, which * group_rows)
+
+    def piece(way, sems, at, sem_at, source, target, step):
         src, dst = way
         send, recv = sems
         return remote(
-            src.at[block(there), span(at)], dst.at[block(landed_at), span(at)], send.at[at], recv.at[at], peer(step)
-        )
-
-    def bulk(way, sems, at, blocks):
-        src, dst = way
-        send, recv = sems
-        return remote(
-            src.at[0 : blocks * HEAD, span(at)], dst.at[0 : blocks * HEAD, span(at)], send.at[at], recv.at[at], peer(1)
-        )
-
-    def send_all(way, sems, at):
+            src.at[source, span(at)], dst.at[target, span(at)], send.at[sem_at], recv.at[sem_at], peer(step)
+        )
+
+    def bulk(way, sems, at, sem_at, blocks):
+        part = slice(0, blocks * HEAD)
+        return piece(way, sems, at, sem_at, part, part, 1)
+
+    def send_out(way, sems, at, sem_at, low, high):
         def body(step, carry):
-            piece(way, sems, at, step, lax.rem(chip + step, EXPERTS), chip).start()
+            there = lax.rem(chip + step, EXPERTS)
+            piece(way, sems, at, sem_at, block(there), spot(step), step).start()
             return carry
 
-        lax.fori_loop(1, EXPERTS, body, 0)
-
-    def wait_all(way, sems, at):
-        bulk(way, sems, at, EXPERTS - 1).wait_recv()
-
-    def wait_sent(way, sems):
-        for at in range(QUARTERS):
-            bulk(way, sems, at, EXPERTS - 1).wait_send()
+        lax.fori_loop(low, high, body, 0)
 
     def keep_own(way, at):
         src, dst = way
-        dst[block(chip), span(at)] = src[block(chip), span(at)]
+        dst[spot(0), span(at)] = src[block(chip), span(at)]
 
     x_way, x_sems = (send_x, x_rows), (x_send, x_recv)
     c_way, c_sems = (send_c, c_rows), (c_send, c_recv)
     b_way, b_sems = (out_rows, back_rows), (b_send, b_recv)
+
+    def either(start, copy_first, copy_second):
+        @pl.when(sec == 0)
+        def _():
+            copy_first.start() if start else copy_first.wait()
+
+        @pl.when(sec == 1)
+        def _():
+            copy_second.start() if start else copy_second.wait()
+
+    def result_out(at, start):
+        cols = columns(at)
+        either(
+            start,
+            pltpu.make_async_copy(landed.at[:, cols], passed_back_hbm.at[:, cols], out_sem.at[1 + at]),
+            pltpu.make_async_copy(landed.at[:, cols], passed_on_hbm.at[:, cols], out_sem.at[1 + at]),
+        )
+
+    def zeros_out(at, start):
+        cols = columns(at)
+        sem = out_sem.at[1 + QUARTERS + at]
+        either(
+            start,
+            pltpu.make_async_copy(nothing, passed_on_hbm.at[:, cols], sem),
+            pltpu.make_async_copy(nothing, passed_back_hbm.at[:, cols], sem),
+        )
 
     own_weights = [
         pltpu.make_async_copy(gate_hbm, gate_w.at[core], w_own_sem.at[0]),
         pltpu.make_async_copy(up_hbm, up_w.at[core], w_own_sem.at[1]),
         pltpu.make_async_copy(down_hbm, down_w.at[core, dp], w_own_sem.at[2]),
-        pltpu.make_async_copy(leak_ref, leak_w.at[core], w_own_sem.at[3]),
+        pltpu.make_async_copy(leak_hbm, leak_w.at[core], w_own_sem.at[3]),
     ]
 
     def sib_weights(half):
@@ -241,7 +286,7 @@
             remote(gate_hbm, gate_w.at[half], w_sib_send.at[0], w_sib_recv.at[0], sibling),
             remote(up_hbm, up_w.at[half], w_sib_send.at[1], w_sib_recv.at[1], sibling),
             remote(down_hbm, down_w.at[half, dp], w_sib_send.at[2], w_sib_recv.at[2], sibling),
-            remote(leak_ref, leak_w.at[half], w_sib_send.at[3], w_sib_recv.at[3], sibling),
+            remote(leak_hbm, leak_w.at[half], w_sib_send.at[3], w_sib_recv.at[3], sibling),
         ]
 
     def down_copy(step, owner):
@@ -259,7 +304,7 @@
 
     prepare(0)
     pl.semaphore_wait(barrier, EXPERTS - 1 + n_dp - 1 + 2 + RUN + RUN * at_edge(depth))
-    send_all(x_way, x_sems, 0)
+    send_out(x_way, x_sems, 0, 0, 1, EXPERTS)
 
     for copy in own_weights:
         copy.start()
@@ -270,17 +315,19 @@
 
     for at in range(1, QUARTERS):
         prepare(at)
-        send_all(x_way, x_sems, at)
-
-    def send_grads(at):
+        send_out(x_way, x_sems, at, at, 1, EXPERTS)
+
+    cot_in.wait()
+
+    group_steps = [(max(1, which * per_group), (which + 1) * per_group) for which in range(GROUPS)]
+    for at in range(QUARTERS):
         store_slots(at, dot(pick, cot_ref[:, columns(at)]) * slot_gate, send_c)
-        send_all(c_way, c_sems, at)
-        keep_own(c_way, at)
-
-    for at in range(QUARTERS // 2):
-        send_grads(at)
+        send_out(c_way, c_sems, at, at, *group_steps[0])
+    for at in range(QUARTERS):
+        send_out(c_way, c_sems, at, QUARTERS + at, *group_steps[1])
     for at in range(QUARTERS):
         keep_own(x_way, at)
+        keep_own(c_way, at)
 
     one = jnp.where(iota((tokens, tokens), 0) == iota((tokens, tokens), 1), 1.0, 0.0)
     inv_row = jnp.sum(one * inv_rms, axis=0, keepdims=True)
@@ -303,6 +350,10 @@
 
     lax.fori_loop(0, EXPERTS, clear, 0)
 
+    nothing[...] = jnp.zeros_like(nothing)
+    for at in range(QUARTERS):
+        zeros_out(at, True)
+
     for copy in own_weights:
         copy.wait()
     for copy in sib_weights(1 - core):
@@ -311,8 +362,9 @@
         copy.wait_send()
 
     for at in range(QUARTERS):
-        wait_all(x_way, x_sems, at)
-        unfold(at, x_rows, unfold_all, rows, slots - rows)
+        bulk(x_way, x_sems, at, at, EXPERTS - 1).wait_recv()
+        for which in range(GROUPS):
+            unfold_slots(which, at, x_rows)
         for half in range(2):
             for weight, total in ((gate_w, gate_act), (up_w, up_act)):
                 part = dot(x_rows[:, heads(at)], weight[half, columns(at), :])
@@ -324,7 +376,7 @@
             part = pl.ds(pl.multiple_of(at * 32, 32), 32)
             gate_in = gate_act[half, part, :]
             up_in = up_act[half, part, :]
-            leak = leak_w[half, 0:1, :]
+            leak = leak_w[half]
             opened = lax.logistic(gate_in)
             silu = gate_in * opened
             drive = silu * up_in
@@ -372,48 +424,47 @@
     def far_place(origin):
         return (origin // RUN) * 2 + origin % 2
 
-    def send_back(at):
+    def send_back(which, at):
         def body(step, carry):
-            there = lax.rem(chip + step, EXPERTS)
-            far = is_far(there, chip)
+            turn = EXPERTS - step
+            far = is_far(lax.rem(chip + turn, EXPERTS), chip)
 
             @pl.when(far == 0)
             def _():
-                piece(b_way, b_sems, at, step, there, chip).start()
+                piece(b_way, b_sems, at, at, block(step), block(chip), turn).start()
 
             @pl.when(far == 1)
             def _():
                 remote(
-                    out_rows.at[block(there), span(at)], far_rows.at[block(far_place(chip)), span(at)],
-                    b_send.at[at], f_recv.at[at], peer(step, 1 - sec),
+                    out_rows.at[block(step), span(at)], far_rows.at[block(far_place(chip)), span(at)],
+                    b_send.at[at], f_recv.at[at], peer(turn, 1 - sec),
                 ).start()
 
             return carry
 
-        lax.fori_loop(1, EXPERTS, body, 0)
-        keep_own(b_way, at)
+        lax.fori_loop(*group_steps[which], body, 0)
+        if which == 0:
+            back_rows[block(chip), span(at)] = out_rows[0:HEAD, span(at)]
 
     def wait_near(at):
         @pl.when(at_edge(depth) == 0)
         def _():
-            bulk(b_way, b_sems, at, EXPERTS - 1).wait_recv()
+            bulk(b_way, b_sems, at, at, EXPERTS - 1).wait_recv()
 
         @pl.when(at_edge(depth) == 1)
         def _():
-            bulk(b_way, b_sems, at, EXPERTS - 1 - far_blocks).wait_recv()
+            bulk(b_way, b_sems, at, at, EXPERTS - 1 - far_blocks).wait_recv()
 
     def wait_far(at):
-        bulk((out_rows, far_rows), (b_send, f_recv), at, far_blocks).wait_recv()
+        bulk((out_rows, far_rows), (b_send, f_recv), at, at, far_blocks).wait_recv()
 
     @pl.when(sec == 0)
     def _():
         for at in range(QUARTERS):
             value = dot(rate[0], down_w[0, at]) + dot(rate[1], down_w[1, at])
-            store_slots(at, value, out_rows)
-            send_back(at)
-
-    for at in range(QUARTERS // 2, QUARTERS):
-        send_grads(at)
+            for which in range(GROUPS):
+                store_group(which, at, value[group(which)], out_rows)
+                send_back(which, at)
 
     meta_copy().wait()
     far_first, far_second, far_both, far_counts = routes(meta_recv[0:2, :], tokens)
@@ -425,55 +476,61 @@
     far_slot = jnp.where(far_head, far_row % HEAD, HEAD + far_row % TAIL)
     far_mix[...] = slots_of(far_expert, far_slot, far_both, far_counts, far_weights)[1].T.astype(BF16)
 
-    for at in range(QUARTERS):
-        wait_all(c_way, c_sems, at)
-        unfold(at, c_rows, unfold_all, rows, slots - rows)
-        for half in range(2):
-            part = dot_t(c_rows[:, heads(at)], down_w[half, at])
-            rate_grad[half] = part if at == 0 else rate_grad[half] + part
-    for half in range(2):
-        gg[half] = (rate_grad[half] * der_gate[half]).astype(BF16)
-        ug[half] = (rate_grad[half] * der_up[half]).astype(BF16)
-
-    def dots_copy(step, there, landed_at):
-        def tile(at):
-            return pl.ds(pl.multiple_of(at * 8, 8), 8)
-
-        return remote(
-            dots.at[tile(there), :], dots_recv.at[tile(landed_at), :], v_send.at[0], v_recv.at[0], peer(step)
-        )
+    def dots_copy(turn, source, target):
+        return remote(dots.at[source, :], dots_recv.at[target, :], v_send.at[0], v_recv.at[0], peer(turn))
+
+    def tile(at):
+        return pl.ds(pl.multiple_of(at * 8, 8), 8)
 
     def dots_bulk():
         part = slice(0, 8 * (EXPERTS - 1))
-        return remote(dots.at[part, :], dots_recv.at[part, :], v_send.at[0], v_recv.at[0], peer(1))
-
-    @pl.when(sec == 1)
-    def _():
+        return dots_copy(1, part, part)
+
+    def send_dots():
+        product = jnp.zeros((slots, 1), F32)
+        for half in range(2):
+            terms = gg[half].astype(F32) * gate_act[half] + ug[half].astype(F32) * up_act[half]
+            product = product + jnp.sum(terms, axis=1, keepdims=True)
+        local_row = iota((slots, tokens), 0) % group_rows
+        local_slot = jnp.where(local_row < group_heads, local_row % HEAD, HEAD + local_row % TAIL)
+        placed = product * jnp.where(local_slot == iota((slots, tokens), 1), 1.0, 0.0)
+        column = iota((8 * EXPERTS, slots), 1)
+        within = column % group_rows
+        source = jnp.where(within < group_heads, within // HEAD, (within - group_heads) // TAIL)
+        source = source + (column // group_rows) * per_group
+        gather = jnp.where(source == iota((8 * EXPERTS, slots), 0) // 8, 1.0, 0.0)
+        dots[...] = jnp.dot(gather, placed, precision=lax.Precision.HIGHEST, preferred_element_type=F32)
+
+        def body(step, carry):
+            dots_copy(EXPERTS - step, tile(step), tile(chip)).start()
+            return carry
+
+        lax.fori_loop(1, EXPERTS, body, 0)
+        dots_recv[tile(chip), :] = dots[0:8, :]
+
+    for which in range(GROUPS):
+        part = group(which)
         for at in range(QUARTERS):
-            value = dot_t(gg[0], gate_w[0, columns(at), :]) + dot_t(gg[1], gate_w[1, columns(at), :])
-            value = value + dot_t(ug[0], up_w[0, columns(at), :]) + dot_t(ug[1], up_w[1, columns(at), :])
-            store_slots(at, value * gain_ref[:, columns(at)], out_rows)
-            if at == 0:
-                product = jnp.zeros((slots, 1), F32)
-                for half in range(2):
-                    terms = gg[half].astype(F32) * gate_act[half] + ug[half].astype(F32) * up_act[half]
-                    product = product + jnp.sum(terms, axis=1, keepdims=True)
-                placed = product * jnp.where(slot_at == iota((slots, tokens), 1), 1.0, 0.0)
-                source_at = iota((8 * EXPERTS, slots), 1)
-                source = jnp.where(source_at < rows, source_at // HEAD, (source_at - rows) // TAIL)
-                group = jnp.where(source == iota((8 * EXPERTS, slots), 0) // 8, 1.0, 0.0)
-                dots[...] = jnp.dot(
-                    group, placed, precision=lax.Precision.HIGHEST, preferred_element_type=F32
-                )
-
-                def body(step, carry):
-                    dots_copy(step, lax.rem(chip + step, EXPERTS), chip).start()
-                    return carry
-
-                lax.fori_loop(1, EXPERTS, body, 0)
-                tile = pl.ds(pl.multiple_of(chip * 8, 8), 8)
-                dots_recv[tile, :] = dots[tile, :]
-            send_back(at)
+            low, high = group_steps[which]
+            bulk(c_way, c_sems, at, which * QUARTERS + at, high - low).wait_recv()
+            unfold_slots(which, at, c_rows)
+            for half in range(2):
+                term = dot_t(c_rows[part, heads(at)], down_w[half, at])
+                rate_grad[half, part, :] = term if at == 0 else rate_grad[half, part, :] + term
+        for half in range(2):
+            gg[half, part, :] = (rate_grad[half, part, :] * der_gate[half, part, :]).astype(BF16)
+            ug[half, part, :] = (rate_grad[half, part, :] * der_up[half, part, :]).astype(BF16)
+
+        @pl.when(sec == 1)
+        def _():
+            for at in range(QUARTERS):
+                cols = columns(at)
+                value = dot_t(gg[0, part, :], gate_w[0, cols, :]) + dot_t(gg[1, part, :], gate_w[1, cols, :])
+                value = value + dot_t(ug[0, part, :], up_w[0, cols, :]) + dot_t(ug[1, part, :], up_w[1, cols, :])
+                store_group(which, at, value * gain_ref[:, cols], out_rows)
+                send_back(which, at)
+                if which == GROUPS - 1 and at == 0:
+                    send_dots()
 
     def sib_copy(step, at):
         part = pl.ds(pl.multiple_of(at * shard, shard), shard)
@@ -489,8 +546,8 @@
     for step in range(n_dp + 1):
         if step < n_dp:
             at = lax.rem(dp + step + 1, n_dp)
-            for piece in range(2):
-                low = piece * halves
+            for side in range(2):
+                low = side * halves
                 part = pl.ds(pl.multiple_of(at * shard + low, halves), halves)
                 normed = x_rows[:, pl.ds(pl.multiple_of(at * pitch + low, LANES), halves)]
                 own_term[step % 2, low : low + halves, :] = t_dot(normed, ug[core])
@@ -545,7 +602,9 @@
     total_grad = sib_recv[own, :].astype(F32)
     for step in range(1, n_dp):
         total_grad = total_grad + rep_recv[step - 1].astype(F32)
-    upgrad_ref[...] = total_grad.astype(BF16)
+    sib_recv[own, :] = total_grad.astype(BF16)
+    grad_out = pltpu.make_async_copy(sib_recv.at[own, :], up_grad_hbm, out_sem.at[0])
+    grad_out.start()
 
     edge = at_edge(depth)
 
@@ -553,7 +612,7 @@
     def _():
         for at in range(QUARTERS):
             pass_copy(at).wait()
-            res_ref[:, columns(at)] = landed[:, columns(at)]
+            result_out(at, True)
 
     @pl.when(edge == 1)
     def _():
@@ -563,11 +622,18 @@
             unfold(at, far_rows, unfold_far, far_heads, far_slots - far_heads)
             direct = dot(far_mix[...], far_rows[:, heads(at)])
             pass_copy(at).wait()
-            res_ref[:, columns(at)] = (landed[:, columns(at)].astype(F32) + direct).astype(BF16)
-
-    wait_sent(x_way, x_sems)
-    wait_sent(c_way, c_sems)
-    wait_sent(b_way, b_sems)
+            landed[:, columns(at)] = (landed[:, columns(at)].astype(F32) + direct).astype(BF16)
+            result_out(at, True)
+
+    for at in range(QUARTERS):
+        zeros_out(at, False)
+        result_out(at, False)
+    grad_out.wait()
+    for at in range(QUARTERS):
+        bulk(x_way, x_sems, at, at, EXPERTS - 1).wait_send()
+        bulk(b_way, b_sems, at, at, EXPERTS - 1).wait_send()
+        for which, (low, high) in enumerate(group_steps):
+            bulk(c_way, c_sems, at, which * QUARTERS + at, high - low).wait_send()
 
     @pl.when(sec == 1)
     def _():
@@ -594,19 +660,23 @@
     def scratch(kind, *shape):
         return pltpu.VMEM(shape, kind)
 
-    result, up_grad = pl.pallas_call(
+    passed_on, passed_back, up_grad = pl.pallas_call(
         kernel,
         out_shape=(
             jax.ShapeDtypeStruct((tokens, width), BF16),
+            jax.ShapeDtypeStruct((tokens, width), BF16),
             jax.ShapeDtypeStruct((shard, hidden), BF16),
         ),
-        in_specs=[vmem] * 6 + [anywhere] * 3,
-        out_specs=(vmem, vmem),
+        in_specs=[vmem] * 3 + [anywhere] * 6,
+        out_specs=(anywhere, anywhere, anywhere),
         scratch_shapes=[
+            scratch(BF16, tokens, width),
+            scratch(BF16, tokens, width),
+            scratch(BF16, tokens, width // QUARTERS),
             scratch(BF16, 2, width, hidden),
             scratch(BF16, 2, width, hidden),
             scratch(BF16, 2, n_dp, hidden, shard),
-            scratch(F32, 2, 8, hidden),
+            scratch(F32, 2, 1, hidden),
             scratch(BF16, rows, pitched),
             scratch(BF16, rows, pitched),
             scratch(BF16, slots, pitched),
@@ -636,28 +706,25 @@
             scratch(BF16, 2, slots, hidden),
             dma((4,)), dma((4,)), dma((4,)),
             dma((n_dp - 1,)), dma((n_dp - 1,)), dma((n_dp - 1,)), dma((n_dp - 1,)),
-            *([dma((QUARTERS,))] * 7),
+            *([dma((QUARTERS,))] * 2), *([dma((GROUPS * QUARTERS,))] * 2), *([dma((QUARTERS,))] * 3),
             dma((QUARTERS,)), dma((QUARTERS,)), dma((n_dp,)), dma((n_dp,)),
             dma((n_dp - 1,)), dma((n_dp - 1,)), dma((1,)), dma((1,)), dma((1,)), dma((1,)),
+            dma((2,)), dma((1 + 2 * QUARTERS,)),
         ],
         compiler_params=pltpu.CompilerParams(
             collective_id=0, has_side_effects=True, vmem_limit_bytes=60 * 2**20
         ),
     )(
-        activations[0],
-        cotangent[0],
         norm_gain,
         route_ids[0].T,
         route_gates[0].T,
-        jnp.broadcast_to(leak_rates, (8, hidden)),
+        activations[0],
+        cotangent[0],
+        leak_rates,
         gate_weight[0],
         up_weight[0],
         down_weight[0],
     )
-    first = lax.axis_index("section") == 0
-    nothing = jnp.zeros_like(result)
-    passed_on = jnp.where(first, nothing, result)
-    passed_back = jnp.where(first, result, nothing)
     return (passed_on[None], passed_back[None], up_grad[None])
 
 

time: 204 us -> 203 us (level)
  local copies, waits for them, and re-layouts: 1.49 us -> 5.53 us
  other arithmetic: 3.46 us -> 0 us
    unnamed x3 -> x5, local copies, waits for them, and re-layouts: 0.88 us -> 5.53 us
    broadcast_in_dim x1 -> x0, other arithmetic: 2.76 us -> none  [per_device(): return (passed_on[None], passed_back[None], up_grad[None])]
where the time goes in v4:
time: 203 us
  Pallas kernels  197 us (97%)
  local copies, waits for them, and re-layouts  5.53 us (3%)
    pallas_call x1, Pallas kernels, per_device(): pl.pallas_call(kernel, out_shape=(jax.ShapeDtypeStruct((tokens, width), B...  197 us
    unnamed x5, local copies, waits for them, and re-layouts  5.53 us

profile of v4, /device:TPU:32, one launch (start us, length us, event | category | flops | bytes accessed | tf_op | source)
XLA Modules:
  0.0 202.8 jit_solution(15167203825951933225)
XLA Ops:
  0.6 196.6 %shard_map.112 = (bf16[128,4096]{1,0:T(8,128)(2,1)}, bf16[128,4096]{1,0:T(8,128)(2,1)}, bf16[1024,384]{1,0:T(8,128)(2,1)}) custom-call(f32[1,4096]{1,0:T(1,128)} %gain_ref.1, s32[2,128]{1,0:T(2,128)} %bitcast.22, f32[2,128]{1,0:T(2,128)} %bitcast.23, bf16[128,4096]{1,0:T(8,128)(2,1)} %bitcast.18, bf16[128,4096]{1,0:T(8,128)(2,1)} %bitcast.19, ...), custom_call_target="tpu_custom_call" | custom-call | tf_op jit(solution)/shard_map/pallas_call | solution.py:663
  197.2 0.0 copy-start
  197.2 2.4 %copy.15 = bf16[1,128,4096]{2,1,0:T(8,128)(2,1)} copy(bf16[1,128,4096]{2,1,0:T(8,128)(2,1)} %bitcast.17) | data formatting | bytes 2097152
  199.6 2.3 %copy.16 = bf16[1,128,4096]{2,1,0:T(8,128)(2,1)} copy(bf16[1,128,4096]{2,1,0:T(8,128)(2,1)} %bitcast.16) | data formatting | bytes 2097152
  201.9 0.0 copy-done
  201.9 0.9 copy.17
Async XLA Ops:
  197.2 4.7 %copy-start = (bf16[1024,384]{1,0:T(8,128)(2,1)S(1)}, bf16[1024,384]{1,0:T(8,128)(2,1)}, u32[]{:S(2)}) copy-start(bf16[1024,384]{1,0:T(8,128)(2,1)} %get-tuple-element.8) | copy-start | bytes 2359300
